TPU v7x, 32 devices: a whole 2x2x4 slice. The times are simulated.
32 devices in a mesh: grp: 2 (over x), row: 16 (over z, y, core).
Axes of the slice: x: 2, y: 2, z: 4, core: 2. Of those that a mesh axis runs over, the one named last changes fastest.
Arguments:
- cell_coeffs: float32 [6, 32, 384], P(None, 'row'), may hold values from 0.5 to 2
- z_factor: float32 [4, 64, 384, 128], P(None, ('grp', 'row')), parts along dimension 1, may hold values from -0.022552745 to 0.022552745
- noise_cols: float32 [4, 64, 384, 128], P(None, ('grp', 'row')), parts along dimension 1, may hold values from -0.022552745 to 0.022552745
- q_bar: float32 [4, 64, 384, 256], P(None, ('grp', 'row')), parts along dimension 1, may hold values from -10 to 10
- r_bar: float32 [512, 256], P('grp'), parts along dimension 0, may hold values from -11.085125 to 11.085125
Outputs:
- z_grad: float32 [4, 64, 384, 128], P(None, ('grp', 'row')), parts along dimension 1
- noise_grad: float32 [4, 64, 384, 128], P(None, ('grp', 'row')), parts along dimension 1
There are 2 independent parts, one for each index of `grp`. A program takes and returns all parts, laid end to end along the dimension named above; an argument that names none is the same for every part. Nothing has to cross between parts.
All inputs are finite; a program needn't handle non-finite values.
Results may differ from a plain program's by a relative error of at most 0.000061.
Values sent between devices are 32-bit elements; how exact they have to be, the bound alone decides.
A program may use at most 64 MiB of HBM per device.

v0:
```python
import functools

import jax
import jax.numpy as jnp
from jax import lax
from jax.experimental import pallas as pl
from jax.experimental.pallas import tpu as pltpu
from jax.sharding import PartitionSpec as P

rate_scales = (0.4, 0.4, 0.1, 0.2, 0.1, 0.1)
exact = lax.Precision.HIGHEST


parts = 4
margin = 8


def step_kernel(count, transposed, coef_ref, value_ref, out_ref, coefs, first, source, source_two, send_low, recv_low, send_high, recv_high):
    rows, cells, cols = value_ref.shape[1:]
    chunk = cells // parts
    me = lax.axis_index("row")
    has_low, has_high = me > 0, me < count - 1

    def link(buffer, stage, piece, upward):
        cut = pl.ds(margin + piece * chunk, chunk)
        sends, recvs = (send_high, recv_high) if upward else (send_low, recv_low)
        slot = stage * parts + piece
        return pltpu.make_async_remote_copy(
            src_ref=buffer.at[:, rows if upward else 1, cut],
            dst_ref=buffer.at[:, 0 if upward else rows + 1, cut],
            send_sem=sends.at[slot],
            recv_sem=recvs.at[slot],
            device_id={"row": me + 1 if upward else me - 1},
            device_id_type=pl.DeviceIdType.MESH,
        )

    def send(buffer, stage, piece):
        @pl.when(has_high)
        def _():
            link(buffer, stage, piece, True).start()

        @pl.when(has_low)
        def _():
            link(buffer, stage, piece, False).start()

    def receive(buffer, stage, piece):
        @pl.when(has_low)
        def _():
            link(buffer, stage, piece, True).wait_recv()

        @pl.when(has_high)
        def _():
            link(buffer, stage, piece, False).wait_recv()

    barrier = pltpu.get_barrier_semaphore()

    @pl.when(has_low)
    def _():
        pl.semaphore_signal(barrier, inc=1, device_id={"row": me - 1}, device_id_type=pl.DeviceIdType.MESH)

    @pl.when(has_high)
    def _():
        pl.semaphore_signal(barrier, inc=1, device_id={"row": me + 1}, device_id_type=pl.DeviceIdType.MESH)

    def coef(kind, row, piece):
        return coefs[kind * rows + row, piece * chunk : (piece + 1) * chunk]

    def at(piece):
        return slice(piece * chunk, (piece + 1) * chunk)

    def inner(piece, shift=0):
        return slice(margin + piece * chunk + shift, margin + (piece + 1) * chunk + shift)

    def spread(kind):
        for row in range(rows):
            index = kind * rows + row
            coefs[index] = jnp.broadcast_to(coef_ref[:, index : index + 1], (cells, cols))

    def fill(buffer, values, piece):
        for row in range(rows):
            for quad in range(2):
                value = values[quad, row, at(piece)]
                if transposed:
                    value = value * coef(5, row, piece)
                buffer[quad, row + 1, inner(piece)] = value

    def zero_rim(buffer):
        for quad in range(2):
            for row in range(rows):
                buffer[quad, row + 1, :margin] = jnp.zeros((margin, cols), jnp.float32)
                buffer[quad, row + 1, margin + cells :] = jnp.zeros((margin, cols), jnp.float32)

        @pl.when(jnp.logical_not(has_low))
        def _():
            buffer[:, 0] = jnp.zeros(buffer.shape[:1] + buffer.shape[2:], jnp.float32)

        @pl.when(jnp.logical_not(has_high))
        def _():
            buffer[:, rows + 1] = jnp.zeros(buffer.shape[:1] + buffer.shape[2:], jnp.float32)

    def local(values, buffer, row, piece):
        xa, pa, xb, pb = [values[quad, row, at(piece)] for quad in range(4)]
        detuning, mech, coupling, cavity, phonon, hopping = [coef(kind, row, piece) for kind in range(6)]
        sums = []
        for quad in range(2):
            total = buffer[quad, row + 1, inner(piece, -1)] + buffer[quad, row + 1, inner(piece, 1)]
            if row > 0:
                total = total + buffer[quad, row, inner(piece)]
            if row < rows - 1:
                total = total + buffer[quad, row + 2, inner(piece)]
            sums.append(total)
        if transposed:
            return (
                -0.5 * cavity * xa + detuning * pa - 2.0 * coupling * pb + sums[1],
                -detuning * xa - 0.5 * cavity * pa - sums[0],
                -2.0 * coupling * pa - mech * pb,
                mech * xb - 0.5 * phonon * pb,
            )
        return (
            -0.5 * cavity * xa - detuning * pa - hopping * sums[1],
            detuning * xa - 0.5 * cavity * pa - 2.0 * coupling * xb + hopping * sums[0],
            mech * pb,
            -mech * xb - 0.5 * phonon * pb - 2.0 * coupling * xa,
        )

    def edges(buffer, piece):
        found = []
        for row, halo in ((0, 0), (rows - 1, rows + 1)):
            light_x, light_p = buffer[0, halo, inner(piece)], buffer[1, halo, inner(piece)]
            if transposed:
                found.append((row, light_p, -light_x))
            else:
                hopping = coef(5, row, piece)
                found.append((row, -hopping * light_p, hopping * light_x))
        return found

    spread(5)
    fill(source, value_ref, 0)

    pl.semaphore_wait(barrier, jnp.where(me > 0, 1, 0) + jnp.where(me < count - 1, 1, 0))

    send(source, 0, 0)
    for piece in range(1, parts):
        fill(source, value_ref, piece)
        send(source, 0, piece)
    zero_rim(source)
    zero_rim(source_two)
    for kind in range(5):
        spread(kind)
    for piece in range(parts):
        for row in range(rows):
            for quad, value in enumerate(local(value_ref, source, row, piece)):
                first[quad, row, at(piece)] = value
    for piece in range(parts):
        receive(source, 0, piece)
        for row, add_x, add_p in edges(source, piece):
            first[0, row, at(piece)] = first[0, row, at(piece)] + add_x
            first[1, row, at(piece)] = first[1, row, at(piece)] + add_p
        fill(source_two, first, piece)
        send(source_two, 1, piece)
    for piece in range(parts):
        for row in range(rows):
            for quad, value in enumerate(local(first, source_two, row, piece)):
                out_ref[quad, row, at(piece)] = (
                    value_ref[quad, row, at(piece)] + first[quad, row, at(piece)] + 0.5 * value
                )
    for piece in range(parts):
        receive(source_two, 1, piece)
        for row, add_x, add_p in edges(source_two, piece):
            out_ref[0, row, at(piece)] = out_ref[0, row, at(piece)] + 0.5 * add_x
            out_ref[1, row, at(piece)] = out_ref[1, row, at(piece)] + 0.5 * add_p
    for stage, buffer in enumerate((source, source_two)):
        for piece in range(parts):

            @pl.when(has_high)
            def _():
                link(buffer, stage, piece, True).wait_send()

            @pl.when(has_low)
            def _():
                link(buffer, stage, piece, False).wait_send()


def second_order(coef_columns, values, transposed):
    count = lax.axis_size("row")
    quads, rows, cells, cols = values.shape
    whole = pl.BlockSpec(memory_space=pltpu.VMEM)
    return pl.pallas_call(
        functools.partial(step_kernel, count, transposed),
        out_shape=jax.ShapeDtypeStruct(values.shape, jnp.float32),
        in_specs=[whole] * 2,
        out_specs=whole,
        scratch_shapes=[
            pltpu.VMEM((coef_columns.shape[1], cells, cols), jnp.float32),
            pltpu.VMEM((quads, rows, cells, cols), jnp.float32),
            pltpu.VMEM((2, rows + 2, cells + 2 * margin, cols), jnp.float32),
            pltpu.VMEM((2, rows + 2, cells + 2 * margin, cols), jnp.float32),
        ]
        + [pltpu.SemaphoreType.DMA((2 * parts,))] * 4,
        compiler_params=pltpu.CompilerParams(
            collective_id=2 if transposed else 1, has_side_effects=True, vmem_limit_bytes=40 * 2**20
        ),
    )(coef_columns, values)


def reduction(count, part_ref, half_in, half_sum, quarter_in, quarter_sum, piece_in, full, send_sem, recv_sem, peer_send, peer_recv, back_send, back_recv):
    rows = part_ref.shape[0]
    peers = count // 4
    half, quarter, piece = rows // 2, rows // 4, rows // count
    me = lax.axis_index("row")
    low, mid, top = lax.rem(me, 2), lax.rem(me // 2, 2), me // 4
    pair = me + 1 - 2 * low
    across = me + 2 - 4 * mid

    def other(step):
        return lax.rem(top + step, peers)

    def copy_to(source, target, sends, recvs, slot, where):
        return pltpu.make_async_remote_copy(
            src_ref=source,
            dst_ref=target,
            send_sem=sends.at[slot],
            recv_sem=recvs.at[slot],
            device_id={"row": where},
            device_id_type=pl.DeviceIdType.MESH,
        )

    first = copy_to(
        part_ref.at[pl.ds(pl.multiple_of((1 - low) * half, 8), half)], half_in, send_sem, recv_sem, 0, pair
    )
    first.start()
    yield
    first.wait()
    half_sum[...] = part_ref[pl.ds(pl.multiple_of(low * half, 8), half)] + half_in[...]
    second = copy_to(
        half_sum.at[pl.ds(pl.multiple_of((1 - mid) * quarter, 8), quarter)], quarter_in, send_sem, recv_sem, 1, across
    )
    second.start()
    yield
    second.wait()
    quarter_sum[...] = half_sum[pl.ds(pl.multiple_of(mid * quarter, 8), quarter)] + quarter_in[...]
    outgoing = [
        copy_to(
            quarter_sum.at[pl.ds(pl.multiple_of(other(step) * piece, 8), piece)],
            piece_in.at[step],
            peer_send,
            peer_recv,
            step,
            other(step) * 4 + lax.rem(me, 4),
        )
        for step in range(1, peers)
    ]
    for copy in outgoing:
        copy.start()
    yield
    total = quarter_sum[pl.ds(pl.multiple_of(top * piece, 8), piece)]
    for step, copy in enumerate(outgoing, 1):
        copy.wait()
        total = total + piece_in[step]
    base = low * half + mid * quarter
    mine = pl.ds(pl.multiple_of(base + top * piece, 8), piece)
    full[mine] = total
    returning = [
        copy_to(full.at[mine], full.at[mine], back_send, back_recv, step, other(step) * 4 + lax.rem(me, 4))
        for step in range(1, peers)
    ]
    for copy in returning:
        copy.start()
    yield
    for copy in returning:
        copy.wait()
    own_quarter = full.at[pl.ds(pl.multiple_of(base, 8), quarter)]
    third = copy_to(own_quarter, own_quarter, send_sem, recv_sem, 2, across)
    third.start()
    yield
    third.wait()
    own_half = full.at[pl.ds(pl.multiple_of(low * half, 8), half)]
    fourth = copy_to(own_half, own_half, send_sem, recv_sem, 3, pair)
    fourth.start()
    yield
    fourth.wait()


def reduction_scratch(count, rows, cols):
    peers = count // 4
    return [
        pltpu.VMEM((rows // 2, cols), jnp.float32),
        pltpu.VMEM((rows // 2, cols), jnp.float32),
        pltpu.VMEM((rows // 4, cols), jnp.float32),
        pltpu.VMEM((rows // 4, cols), jnp.float32),
        pltpu.VMEM((peers, rows // count, cols), jnp.float32),
        pltpu.VMEM((rows, cols), jnp.float32),
        pltpu.SemaphoreType.DMA((4,)),
        pltpu.SemaphoreType.DMA((4,)),
    ] + [pltpu.SemaphoreType.DMA((peers,))] * 4


tile = 32


def tile_inverse(block):
    shape = (tile, tile)
    row_ids = lax.broadcasted_iota(jnp.int32, shape, 0)
    col_ids = lax.broadcasted_iota(jnp.int32, shape, 1)
    right = (row_ids == col_ids).astype(jnp.float32)
    left = block
    scale = jnp.zeros(shape, jnp.float32)
    for start in range(0, tile, 8):
        columns = [
            jnp.broadcast_to(left[start:, start + k : start + k + 1], (tile - start, tile)) for k in range(8)
        ]
        below_left, below_right = left[start:], right[start:]
        ids = row_ids[start:]
        for j in range(8):
            pivot = columns[j][j : j + 1]
            factor = jnp.where(ids > start + j, columns[j] * (1.0 / pivot), 0.0)
            scale = jnp.where(row_ids == start + j, lax.rsqrt(pivot), scale)
            for k in range(j + 1, 8):
                columns[k] = columns[k] - factor * columns[k][j : j + 1]
            below_left = below_left - factor * below_left[j : j + 1]
            below_right = below_right - factor * below_right[j : j + 1]
        if start:
            left = jnp.concatenate([left[:start], below_left], axis=0)
            right = jnp.concatenate([right[:start], below_right], axis=0)
        else:
            left, right = below_left, below_right
    return right * scale


def mul(a, b, contract):
    return lax.dot_general(a, b, ((contract[0:1], contract[1:2]), ((), ())), precision=exact, preferred_element_type=jnp.float32)


def sum_kernel(count, product_ref, gram_ref, cross_ref, gram_part, cross_part, *scratch):
    size = gram_ref.shape[0]
    side = size // 2
    gram_scratch, cross_scratch = scratch[:12], scratch[12:]
    gram_full, cross_full = gram_scratch[5], cross_scratch[5]
    me = lax.axis_index("row")
    low, mid, top = lax.rem(me, 2), lax.rem(me // 2, 2), me // 4
    peers = count // 4
    barrier = pltpu.get_barrier_semaphore()
    friends = [me + 1 - 2 * low, me + 2 - 4 * mid]
    friends += [lax.rem(top + step, peers) * 4 + lax.rem(me, 4) for step in range(1, peers)]
    for friend in friends:
        pl.semaphore_signal(barrier, inc=1, device_id={"row": friend}, device_id_type=pl.DeviceIdType.MESH)
    gram_part[:side] = product_ref[:side, :side]
    gram_part[side:size] = product_ref[side:size, :side]
    gram_part[size : size + side] = product_ref[side:size, side:]
    if gram_part.shape[0] > size + side:
        gram_part[size + side :] = jnp.zeros((gram_part.shape[0] - size - side, side), jnp.float32)
    cross_part[:size] = product_ref[size:, :side]
    cross_part[size:] = product_ref[size:, side:]
    pl.semaphore_wait(barrier, len(friends))
    gram_steps = reduction(count, gram_part, *gram_scratch)
    cross_steps = reduction(count, cross_part, *cross_scratch)
    for _ in range(7):
        next(gram_steps, None)
        next(cross_steps, None)
    gram_ref[:side, :side] = gram_full[:side]
    gram_ref[side:, :side] = gram_full[side:size]
    gram_ref[:side, side:] = gram_full[side:size].T
    gram_ref[side:, side:] = gram_full[size : size + side]
    cross_ref[:, :side] = cross_full[:size]
    cross_ref[:, side:] = cross_full[size:]


def device_sum(products):
    count = lax.axis_size("row")
    size = products.shape[1]
    side = size // 2
    unit = 8 * count
    gram_rows = (size + side + unit - 1) // unit * unit
    shape = jax.ShapeDtypeStruct((size, size), jnp.float32)
    whole = pl.BlockSpec(memory_space=pltpu.VMEM)
    return pl.pallas_call(
        functools.partial(sum_kernel, count),
        out_shape=(shape, shape),
        in_specs=[whole],
        out_specs=(whole, whole),
        scratch_shapes=[
            pltpu.VMEM((gram_rows, side), jnp.float32),
            pltpu.VMEM((2 * size, side), jnp.float32),
        ]
        + reduction_scratch(count, gram_rows, side)
        + reduction_scratch(count, 2 * size, side),
        compiler_params=pltpu.CompilerParams(collective_id=0, has_side_effects=True, vmem_limit_bytes=24 * 2**20),
    )(products)


def factor_kernel(gram_ref, cross_ref, bar_ref, inv_ref, mix_ref, work):
    size = gram_ref.shape[0]
    row_ids = lax.broadcasted_iota(jnp.int32, (size, size), 0)
    col_ids = lax.broadcasted_iota(jnp.int32, (size, size), 1)
    work[:, :size] = gram_ref[...]
    work[:, size:] = (row_ids == col_ids).astype(jnp.float32)
    for start in range(0, size, tile):
        stop = start + tile
        small = tile_inverse(work[start:stop, start:stop])
        panel = mul(small, work[start:stop, :], (1, 0))
        work[start:stop, :] = panel
        if stop < size:
            base, end = stop // 128 * 128, size + (stop + 127) // 128 * 128
            update = mul(panel[:, base:size].T, panel[:, base:end], (1, 0))
            work[stop:, base:end] = work[stop:, base:end] - update[stop - base :]
    upper = jnp.where(row_ids <= col_ids, work[:, :size], 0.0)
    inverse = jnp.where(row_ids >= col_ids, work[:, size:], 0.0)
    inv_ref[...] = inverse
    bar = jnp.where(row_ids <= col_ids, bar_ref[...], 0.0)
    middle = mul(upper, bar, (1, 1)) - mul(cross_ref[...], inverse, (1, 1))
    symmetric = jnp.where(row_ids >= col_ids, middle, middle.T)
    mix_ref[...] = mul(inverse.T, mul(symmetric, inverse, (1, 0)), (1, 0))


def factor(gram, cross, r_bar):
    size = gram.shape[0]
    shape = jax.ShapeDtypeStruct((size, size), jnp.float32)
    whole = pl.BlockSpec(memory_space=pltpu.VMEM)
    return pl.pallas_call(
        factor_kernel,
        out_shape=(shape, shape),
        in_specs=[whole] * 3,
        out_specs=(whole, whole),
        scratch_shapes=[pltpu.VMEM((size, 2 * size), jnp.float32)],
        compiler_params=pltpu.CompilerParams(vmem_limit_bytes=24 * 2**20),
    )(gram, cross, r_bar)


def halves(value):
    high = value.astype(jnp.bfloat16)
    return high, (value - high.astype(jnp.float32)).astype(jnp.bfloat16)


def three(left, high, low):
    left_high, left_low = halves(left)
    dot = functools.partial(jnp.dot, preferred_element_type=jnp.float32)
    return dot(left_high, high) + (dot(left_high, low) + dot(left_low, high))


def grad_kernel(bar_ref, z_ref, noise_ref, inv_ref, mix_ref, z_out, noise_out, inv_high, inv_low, mix_high, mix_low):
    @pl.when(pl.program_id(0) == 0)
    def _():
        inv_high[...], inv_low[...] = halves(inv_ref[...])
        mix_high[...], mix_low[...] = halves(mix_ref[...])

    stacked = jnp.concatenate([z_ref[...], noise_ref[...]], axis=1)
    grad = three(bar_ref[...], inv_high[...], inv_low[...]) + three(stacked, mix_high[...], mix_low[...])
    z_out[...] = grad[:, : z_out.shape[1]]
    noise_out[...] = grad[:, z_out.shape[1] :]


def gradient(bar_rows, z_rows, noise_rows, inverse, mix):
    rows, size = bar_rows.shape
    block = rows // 8
    square = pl.BlockSpec((size, size), lambda i: (0, 0))

    def strip(value):
        return pl.BlockSpec((block, value.shape[1]), lambda i: (i, 0))

    return pl.pallas_call(
        grad_kernel,
        grid=(8,),
        out_shape=(
            jax.ShapeDtypeStruct(z_rows.shape, jnp.float32),
            jax.ShapeDtypeStruct(noise_rows.shape, jnp.float32),
        ),
        in_specs=[strip(bar_rows), strip(z_rows), strip(noise_rows), square, square],
        out_specs=(strip(z_rows), strip(noise_rows)),
        scratch_shapes=[pltpu.VMEM((size, size), jnp.bfloat16)] * 4,
        compiler_params=pltpu.CompilerParams(vmem_limit_bytes=24 * 2**20),
    )(bar_rows, z_rows, noise_rows, inverse, mix)


def on_device(cell_coeffs, z_factor, noise_cols, q_bar, r_bar):
    scaled = cell_coeffs * jnp.array(rate_scales, jnp.float32)[:, None, None]
    rank_cols = z_factor.shape[3]
    coef_columns = scaled.reshape(-1, scaled.shape[2]).T

    z_rows = second_order(coef_columns, z_factor, False).reshape(-1, rank_cols)
    noise_rows = noise_cols.reshape(-1, noise_cols.shape[3])
    flat_rows = jnp.concatenate([z_rows, noise_rows], axis=1)
    bar_rows = q_bar.reshape(-1, q_bar.shape[3])
    both = jnp.concatenate([flat_rows, bar_rows], axis=1)
    products = lax.dot_general(both, flat_rows, (((0,), (0,)), ((), ())), precision=lax.Precision.HIGH)
    gram, cross = device_sum(products)
    inverse, mix = factor(gram, cross, r_bar)
    z_part, noise_part = gradient(bar_rows, z_rows, noise_rows, inverse, mix)
    z_grad = second_order(coef_columns, z_part.reshape(z_factor.shape), True)
    return (z_grad, noise_part.reshape(noise_cols.shape))


def solution(mesh):
    return jax.shard_map(
        on_device,
        mesh=mesh,
        in_specs=(
            P(None, "row", None),
            P(None, ("grp", "row"), None, None),
            P(None, ("grp", "row"), None, None),
            P(None, ("grp", "row"), None, None),
            P("grp", None),
        ),
        out_specs=(P(None, ("grp", "row"), None, None), P(None, ("grp", "row"), None, None)),
        check_vma=False,
    )
```

profile of v0, /device:TPU:9, one launch (start us, length us, event | category | flops | bytes accessed | tf_op | source)
XLA Modules:
  0.0 90.8 jit_solution(1182639315638607438)
XLA Ops:
  0.6 0.0 copy-start
  0.6 1.0 %broadcast_multiply_fusion = f32[6,2,384]{2,1,0:T(2,128)S(1)} fusion(f32[6,2,384]{2,1,0:T(2,128)} %param.6, f32[6]{0:T(128)} %constant.2.clone), kind=kLoop, calls=%fused_computation.9 | loop fusion | flops 4608 | bytes 36888 | tf_op jit(solution)/shard_map/mul | solution.py:475
  1.6 0.1 copy.9
  1.8 0.0 copy-start.1
  1.8 1.4 %copy-done.1 = f32[4,2,384,128]{3,2,1,0:T(8,128)S(1)} copy-done((f32[4,2,384,128]{3,2,1,0:T(8,128)S(1)}, f32[4,2,384,128]{3,2,1,0:T(8,128)}, u32[]{:S(2)}) %copy-start.1) | copy-done | bytes 1572888
  3.2 20.4 %shard_map.77 = f32[4,2,384,128]{3,2,1,0:T(8,128)S(1)} custom-call(f32[384,12]{1,0:T(8,128)S(1)} %bitcast.10, f32[4,2,384,128]{3,2,1,0:T(8,128)S(1)} %copy-done.1), custom_call_target="tpu_custom_call" | custom-call | tf_op jit(solution)/shard_map/pallas_call | solution.py:188
  23.6 0.0 copy-done
  23.6 0.0 copy-start.3
  23.6 0.0 copy-start.2
  23.6 7.2 %fusion.product_ref = f32[512,256]{1,0:T(8,128)S(1)} fusion(f32[3072,256]{1,0:T(8,128)S(1)} %bitcast.8, f32[3072,128]{1,0:T(8,128)} %bitcast.13, f32[3072,128]{1,0:T(8,128)S(1)} %bitcast.6), kind=kOutput, calls=%fused_computation | convolution fusion | flops 2419851264 | bytes 6815744 | tf_op jit(solution)/shard_map/dot_general | solution.py:484
  30.8 20.8 %shard_map.78 = (f32[256,256]{1,0:T(8,128)S(1)}, f32[256,256]{1,0:T(8,128)S(1)}) custom-call(f32[512,256]{1,0:T(8,128)S(1)} %fusion.product_ref), custom_call_target="tpu_custom_call" | custom-call | tf_op jit(solution)/shard_map/pallas_call | solution.py:376
  51.6 0.0 copy-done.3
  51.7 12.5 %shard_map.79 = (f32[256,256]{1,0:T(8,128)S(1)}, f32[256,256]{1,0:T(8,128)S(1)}) custom-call(f32[256,256]{1,0:T(8,128)S(1)} %get-tuple-element.8.gram_ref, f32[256,256]{1,0:T(8,128)S(1)} %get-tuple-element.9.cross_ref, f32[256,256]{1,0:T(8,128)S(1)} %copy-done.3), custom_call_target="tpu_custom_call" | custom-call | tf_op jit(solution)/shard_map/pallas_call | solution.py:419
  64.2 0.0 copy-done.2
  64.2 5.3 %shard_map.80 = (f32[3072,128]{1,0:T(8,128)S(1)}, f32[3072,128]{1,0:T(8,128)}) custom-call(f32[3072,256]{1,0:T(8,128)S(1)} %bitcast.9, f32[3072,128]{1,0:T(8,128)S(1)} %bitcast.7, f32[3072,128]{1,0:T(8,128)S(1)} %bitcast.14, f32[256,256]{1,0:T(8,128)S(1)} %get-tuple-element.10.inv_ref, f32[256,256]{1,0:T(8,128)S(1)} %get-tuple-element.11.mix_ref), custom_call_target="tpu_custom_call" | custom-call | tf_op jit(solution)/shard_map/pallas_call | solution.py:460
  69.4 20.2 %shard_map.81 = f32[4,2,384,128]{3,2,1,0:T(8,128)S(1)} custom-call(f32[384,12]{1,0:T(8,128)S(1)} %bitcast.11, f32[4,2,384,128]{3,2,1,0:T(8,128)S(1)} %bitcast.12), custom_call_target="tpu_custom_call" | custom-call | tf_op jit(solution)/shard_map/pallas_call | solution.py:188
  89.6 1.1 %copy.11 = f32[4,2,384,128]{3,2,1,0:T(8,128)} copy(f32[4,2,384,128]{3,2,1,0:T(8,128)S(1)} %shard_map.81) | data formatting | bytes 3145728
  (1 shorter events, 0.0 us)
Async XLA Ops:
  0.6 23.0 %copy-start = (f32[4,2,384,256]{3,2,1,0:T(8,128)S(1)}, f32[4,2,384,256]{3,2,1,0:T(8,128)}, u32[]{:S(2)}) copy-start(f32[4,2,384,256]{3,2,1,0:T(8,128)} %param.9) | copy-start | bytes 9437188
  1.8 1.4 %copy-start.1 = (f32[4,2,384,128]{3,2,1,0:T(8,128)S(1)}, f32[4,2,384,128]{3,2,1,0:T(8,128)}, u32[]{:S(2)}) copy-start(f32[4,2,384,128]{3,2,1,0:T(8,128)} %value_ref.1) | copy-start | bytes 4718596
  23.6 28.0 %copy-start.3 = (f32[256,256]{1,0:T(8,128)S(1)}, f32[256,256]{1,0:T(8,128)}, u32[]{:S(2)}) copy-start(f32[256,256]{1,0:T(8,128)} %bar_ref.1) | copy-start | bytes 786436
  23.6 40.5 %copy-start.2 = (f32[4,2,384,128]{3,2,1,0:T(8,128)S(1)}, f32[4,2,384,128]{3,2,1,0:T(8,128)}, u32[]{:S(2)}) copy-start(f32[4,2,384,128]{3,2,1,0:T(8,128)} %param.8) | copy-start | bytes 4718596
where the time goes:
time: 91.7 us; the launch traced here: 90.8 us
  Pallas kernels  79.2 us (86%)
  matrix products  7.16 us (8%)
  local copies, waits for them, and re-layouts  2.72 us (3%)
  other arithmetic  0.95 us (1%)
    pallas_call x2, Pallas kernels, second_order(): pl.pallas_call(functools.partial(step_kernel, count, transposed), out_sha...  40.6 us
    pallas_call x1, Pallas kernels, device_sum(): pl.pallas_call(functools.partial(sum_kernel, count), out_shape=(shape, sh...  20.8 us
    pallas_call x1, Pallas kernels, factor(): pl.pallas_call(factor_kernel, out_shape=(shape, shape), in_specs=[whole]...  12.5 us
    dot_general x1, matrix products, on_device(): lax.dot_general(both, flat_rows, (((0,), (0,)), ((), ())), precision=lax....  7.16 us
    pallas_call x1, Pallas kernels, gradient(): pl.pallas_call(grad_kernel, grid=(8,), out_shape=(jax.ShapeDtypeStruct(z_...  5.27 us
    unnamed x9, local copies, waits for them, and re-layouts  2.57 us

commit v1 on v0

v1 whole, which is shorter than its diff:
```python
import functools

import jax
import jax.numpy as jnp
from jax import lax
from jax.experimental import pallas as pl
from jax.experimental.pallas import tpu as pltpu
from jax.sharding import PartitionSpec as P

rate_scales = (0.4, 0.4, 0.1, 0.2, 0.1, 0.1)
extra_scales = (1.0, 1.0, 2.0, 0.5, 0.5, 1.0)
exact = lax.Precision.HIGHEST

parts = 6
margin = 8
lag = 2
tile = 32


def reduction(count, part_ref, half_in, half_sum, quarter_in, quarter_sum, piece_in, full, send_sem, recv_sem, peer_send, peer_recv, back_send, back_recv):
    rows = part_ref.shape[0]
    peers = count // 4
    half, quarter, piece = rows // 2, rows // 4, rows // count
    me = lax.axis_index("row")
    low, mid, top = lax.rem(me, 2), lax.rem(me // 2, 2), me // 4
    pair = me + 1 - 2 * low
    across = me + 2 - 4 * mid

    def other(step):
        return lax.rem(top + step, peers)

    def copy_to(source, target, sends, recvs, slot, where):
        return pltpu.make_async_remote_copy(
            src_ref=source,
            dst_ref=target,
            send_sem=sends.at[slot],
            recv_sem=recvs.at[slot],
            device_id={"row": where},
            device_id_type=pl.DeviceIdType.MESH,
        )

    first = copy_to(
        part_ref.at[pl.ds(pl.multiple_of((1 - low) * half, 8), half)], half_in, send_sem, recv_sem, 0, pair
    )
    first.start()
    yield
    first.wait()
    half_sum[...] = part_ref[pl.ds(pl.multiple_of(low * half, 8), half)] + half_in[...]
    second = copy_to(
        half_sum.at[pl.ds(pl.multiple_of((1 - mid) * quarter, 8), quarter)], quarter_in, send_sem, recv_sem, 1, across
    )
    second.start()
    yield
    second.wait()
    quarter_sum[...] = half_sum[pl.ds(pl.multiple_of(mid * quarter, 8), quarter)] + quarter_in[...]
    outgoing = [
        copy_to(
            quarter_sum.at[pl.ds(pl.multiple_of(other(step) * piece, 8), piece)],
            piece_in.at[step],
            peer_send,
            peer_recv,
            step,
            other(step) * 4 + lax.rem(me, 4),
        )
        for step in range(1, peers)
    ]
    for copy in outgoing:
        copy.start()
    yield
    total = quarter_sum[pl.ds(pl.multiple_of(top * piece, 8), piece)]
    for step, copy in enumerate(outgoing, 1):
        copy.wait()
        total = total + piece_in[step]
    base = low * half + mid * quarter
    mine = pl.ds(pl.multiple_of(base + top * piece, 8), piece)
    full[mine] = total
    returning = [
        copy_to(full.at[mine], full.at[mine], back_send, back_recv, step, other(step) * 4 + lax.rem(me, 4))
        for step in range(1, peers)
    ]
    for copy in returning:
        copy.start()
    yield
    for copy in returning:
        copy.wait()
    own_quarter = full.at[pl.ds(pl.multiple_of(base, 8), quarter)]
    third = copy_to(own_quarter, own_quarter, send_sem, recv_sem, 2, across)
    third.start()
    yield
    third.wait()
    own_half = full.at[pl.ds(pl.multiple_of(low * half, 8), half)]
    fourth = copy_to(own_half, own_half, send_sem, recv_sem, 3, pair)
    fourth.start()
    yield
    fourth.wait()


def reduction_scratch(count, rows, cols):
    peers = count // 4
    return [
        pltpu.VMEM((rows, cols), jnp.float32),
        pltpu.VMEM((rows // 2, cols), jnp.float32),
        pltpu.VMEM((rows // 2, cols), jnp.float32),
        pltpu.VMEM((rows // 4, cols), jnp.float32),
        pltpu.VMEM((rows // 4, cols), jnp.float32),
        pltpu.VMEM((peers, rows // count, cols), jnp.float32),
        pltpu.VMEM((rows, cols), jnp.float32),
        pltpu.SemaphoreType.DMA((4,)),
        pltpu.SemaphoreType.DMA((4,)),
    ] + [pltpu.SemaphoreType.DMA((peers,))] * 4


def tile_inverse(block):
    shape = (tile, tile)
    row_ids = lax.broadcasted_iota(jnp.int32, shape, 0)
    col_ids = lax.broadcasted_iota(jnp.int32, shape, 1)
    right = (row_ids == col_ids).astype(jnp.float32)
    left = block
    scale = jnp.zeros(shape, jnp.float32)
    for start in range(0, tile, 8):
        columns = [
            jnp.broadcast_to(left[start:, start + k : start + k + 1], (tile - start, tile)) for k in range(8)
        ]
        below_left, below_right = left[start:], right[start:]
        ids = row_ids[start:]
        for j in range(8):
            pivot = columns[j][j : j + 1]
            factor = jnp.where(ids > start + j, columns[j] * (1.0 / pivot), 0.0)
            scale = jnp.where(row_ids == start + j, lax.rsqrt(pivot), scale)
            for k in range(j + 1, 8):
                columns[k] = columns[k] - factor * columns[k][j : j + 1]
            below_left = below_left - factor * below_left[j : j + 1]
            below_right = below_right - factor * below_right[j : j + 1]
        if start:
            left = jnp.concatenate([left[:start], below_left], axis=0)
            right = jnp.concatenate([right[:start], below_right], axis=0)
        else:
            left, right = below_left, below_right
    return right * scale


def mul(a, b, contract):
    return lax.dot_general(a, b, ((contract[0:1], contract[1:2]), ((), ())), precision=exact, preferred_element_type=jnp.float32)


def dot16(a, b, contract):
    return lax.dot_general(a, b, ((contract[0:1], contract[1:2]), ((), ())), preferred_element_type=jnp.float32)


def halves(value):
    high = value.astype(jnp.bfloat16)
    return high, (value - high.astype(jnp.float32)).astype(jnp.bfloat16)


def whole_kernel(
    count, coef_ref, z_hbm, noise_hbm, bar_hbm, rbar_ref, z_out, noise_out,
    coef_rows, halo_rows, coefs, values, hop, second, first, partial, light, halo,
    noise_in, bar_in, all_high, all_low, acc_z, acc_n, work, weight_z, weight_n,
    load_sem, send_low, recv_low, send_high, recv_high, *sums,
):
    quads, rows, cells, cols = z_hbm.shape
    size = 2 * cols
    chunk = cells // parts
    strips = quads * rows
    block = strips * chunk
    me = lax.axis_index("row")
    has_low, has_high = me > 0, me < count - 1
    gram_scratch, cross_scratch = sums[:13], sums[13:]
    gram_part, gram_full = gram_scratch[0], gram_scratch[6]
    cross_part, cross_full = cross_scratch[0], cross_scratch[6]

    load_z = pltpu.make_async_copy(z_hbm, values.at[:, :, margin : margin + cells], load_sem.at[0])
    load_noise = pltpu.make_async_copy(noise_hbm, noise_in, load_sem.at[1])
    load_bar = pltpu.make_async_copy(bar_hbm, bar_in, load_sem.at[2])
    load_z.start()

    barrier = pltpu.get_barrier_semaphore()
    peers = count // 4
    low, mid, top = lax.rem(me, 2), lax.rem(me // 2, 2), me // 4
    friends = [me + 1 - 2 * low, me + 2 - 4 * mid]
    friends += [lax.rem(top + step, peers) * 4 + lax.rem(me, 4) for step in range(1, peers)]

    @pl.when(has_low)
    def _():
        pl.semaphore_signal(barrier, inc=1, device_id={"row": me - 1}, device_id_type=pl.DeviceIdType.MESH)

    @pl.when(has_high)
    def _():
        pl.semaphore_signal(barrier, inc=1, device_id={"row": me + 1}, device_id_type=pl.DeviceIdType.MESH)

    for friend in friends:
        pl.semaphore_signal(barrier, inc=1, device_id={"row": friend}, device_id_type=pl.DeviceIdType.MESH)
    load_noise.start()
    load_bar.start()

    def link(source, target, slot, upward):
        sends, recvs = (send_high, recv_high) if upward else (send_low, recv_low)
        return pltpu.make_async_remote_copy(
            src_ref=source,
            dst_ref=target,
            send_sem=sends.at[slot],
            recv_sem=recvs.at[slot],
            device_id={"row": me + 1 if upward else me - 1},
            device_id_type=pl.DeviceIdType.MESH,
        )

    def message(source, padded, run, stage, piece, upward):
        offset = margin if padded else 0
        return link(
            source.at[0:2, rows - 1 if upward else 0, pl.ds(offset + piece * chunk, chunk)],
            halo.at[run, 0 if upward else 1, 2 * stage : 2 * stage + 2, pl.ds(piece * chunk, chunk)],
            (2 * run + stage) * parts + piece,
            upward,
        )

    def rates(upward):
        return link(coef_rows.at[8:16], halo_rows.at[0 if upward else 1], 4 * parts, upward)

    def send(copy_of):
        @pl.when(has_high)
        def _():
            copy_of(True).start()

        @pl.when(has_low)
        def _():
            copy_of(False).start()

    def receive(copy_of):
        @pl.when(has_low)
        def _():
            copy_of(True).wait_recv()

        @pl.when(has_high)
        def _():
            copy_of(False).wait_recv()

    def sent(copy_of):
        @pl.when(has_high)
        def _():
            copy_of(True).wait_send()

        @pl.when(has_low)
        def _():
            copy_of(False).wait_send()

    def at(piece):
        return slice(piece * chunk, (piece + 1) * chunk)

    def inner(piece, shift=0):
        return slice(margin + piece * chunk + shift, margin + (piece + 1) * chunk + shift)

    def coef(kind, row, piece):
        return coefs[kind * rows + row, at(piece)]

    def strip(piece, quad, row):
        start = piece * block + (quad * rows + row) * chunk
        return slice(start, start + chunk)

    for kind in range(6):
        for row in range(rows):
            line = coef_ref[kind, row : row + 1] * jnp.float32(rate_scales[kind])
            coef_rows[kind * rows + row : kind * rows + row + 1] = line * jnp.float32(extra_scales[kind])
    coef_rows[12:16] = jnp.zeros((4, cells), jnp.float32)
    columns = coef_rows[...].T
    for index in range(6 * rows):
        coefs[index] = jnp.broadcast_to(columns[:, index : index + 1], (cells, cols))
    for buffer in (values, hop, second):
        for quad in range(2):
            for row in range(rows):
                buffer[quad, row, :margin] = jnp.zeros((margin, cols), jnp.float32)
                buffer[quad, row, margin + cells :] = jnp.zeros((margin, cols), jnp.float32)
    for side, has in enumerate((has_low, has_high)):

        @pl.when(jnp.logical_not(has))
        def _():
            halo[:, side] = jnp.zeros(halo.shape[:1] + halo.shape[2:], jnp.float32)
            halo_rows[side] = jnp.zeros(halo_rows.shape[1:], jnp.float32)

    def local(get, buffer, row, piece, transposed):
        xa, pa, xb, pb = [get(quad, row, piece) for quad in range(4)]
        detuning, mech, coupling, cavity, phonon, hopping = [coef(kind, row, piece) for kind in range(6)]
        hops = [
            buffer[quad, row, inner(piece, -1)] + buffer[quad, row, inner(piece, 1)] + buffer[quad, 1 - row, inner(piece)]
            for quad in range(2)
        ]
        if transposed:
            return (
                detuning * pa - cavity * xa - coupling * pb + hops[1],
                -detuning * xa - cavity * pa - hops[0],
                -coupling * pa - mech * pb,
                mech * xb - phonon * pb,
            )
        return (
            -cavity * xa - detuning * pa - hopping * hops[1],
            detuning * xa - cavity * pa - coupling * xb + hopping * hops[0],
            mech * pb,
            -mech * xb - phonon * pb - coupling * xa,
        )

    def value_at(quad, row, piece):
        return values[quad, row, inner(piece)]

    def first_at(quad, row, piece):
        return first[quad, row, at(piece)]

    def first_term(run, source, piece):
        for row in range(rows):
            for quad, value in enumerate(local(value_at, source, row, piece, run == 1)):
                first[quad, row, at(piece)] = value
                if quad < 2:
                    partial[quad, row, at(piece)] = coef(5, row, piece) * value if run else value
        send(functools.partial(message, partial, False, run, 1, piece))

    def first_halo(run, source, piece):
        receive(functools.partial(message, source, True, run, 0, piece))
        for row in range(rows):
            halo_x, halo_p = halo[run, row, 0, at(piece)], halo[run, row, 1, at(piece)]
            hopping = coef(5, row, piece)
            if run:
                new_x, new_p = first_at(0, row, piece) + halo_p, first_at(1, row, piece) - halo_x
            else:
                new_x = first_at(0, row, piece) - hopping * halo_p
                new_p = first_at(1, row, piece) + hopping * halo_x
            first[0, row, at(piece)] = new_x
            first[1, row, at(piece)] = new_p
            second[0, row, inner(piece)] = hopping * new_x if run else new_x
            second[1, row, inner(piece)] = hopping * new_p if run else new_p

    def second_term(run, row, piece):
        found = local(first_at, second, row, piece, run == 1)
        return [value_at(quad, row, piece) + first_at(quad, row, piece) + 0.5 * found[quad] for quad in range(4)]

    def last_halo(run, source, piece):
        receive(functools.partial(message, partial, False, run, 1, piece))
        found = []
        for row in range(rows):
            beyond = coefs[6 * rows + row, at(piece)]
            own_x, own_p = source[0, row, inner(piece)], source[1, row, inner(piece)]
            halo_x, halo_p = halo[run, row, 2, at(piece)], halo[run, row, 3, at(piece)]
            if run:
                add_x, add_p = 0.5 * (halo_p - beyond * own_x), -0.5 * (halo_x + beyond * own_p)
            else:
                hopping = 0.5 * coef(5, row, piece)
                add_x, add_p = -hopping * (halo_p + beyond * own_x), hopping * (halo_x - beyond * own_p)
            found.append((add_x, add_p))
        return found

    pl.semaphore_wait(barrier, jnp.where(me > 0, 1, 0) + jnp.where(me < count - 1, 1, 0) + len(friends))
    send(rates)
    load_z.wait()
    for piece in range(parts):
        send(functools.partial(message, values, True, 0, 0, piece))
    for piece in range(parts):
        first_term(0, values, piece)

    load_noise.wait()
    load_bar.wait()
    for piece in range(parts):
        for quad in range(quads):
            for row in range(rows):
                where = strip(piece, quad, row)
                all_high[where, cols:size], all_low[where, cols:size] = halves(noise_in[quad, row, at(piece)])
                all_high[where, size:], all_low[where, size:] = halves(bar_in[quad, row, at(piece)])

    def accumulate(acc, start, stop, begin, fresh):
        lines = slice(start, stop)
        high = all_high[lines, begin : begin + cols]
        left = jnp.concatenate([high, all_low[lines, begin : begin + cols]], axis=1)
        both = dot16(left, all_high[lines, begin:], (0, 0))
        found = both[:cols] + both[cols:] + dot16(high, all_low[lines, begin:], (0, 0))
        acc[...] = found if fresh else acc[...] + found

    for piece in range(parts):
        accumulate(acc_n, piece * block, (piece + 1) * block, cols, piece == 0)

    receive(rates)
    sides = [halo_rows[0].T, halo_rows[1].T]
    for side in range(2):
        index = 10 - 8 + (rows - 1 if side == 0 else 0)
        coefs[6 * rows + side] = jnp.broadcast_to(sides[side][:, index : index + 1], (cells, cols))

    def finish(piece):
        for row in range(rows):
            found = second_term(0, row, piece)
            for quad in range(2):
                light[quad, row, at(piece)] = found[quad]
            for quad in range(2, 4):
                where = strip(piece, quad, row)
                all_high[where, :cols], all_low[where, :cols] = halves(found[quad])
        accumulate(acc_z, piece * block + block // 2, (piece + 1) * block, 0, piece == 0)

    for piece in range(parts):
        first_halo(0, values, piece)
        if piece:
            finish(piece - 1)
    finish(parts - 1)
    for piece in range(parts):
        for row, added in enumerate(last_halo(0, values, piece)):
            for quad in range(2):
                where = strip(piece, quad, row)
                all_high[where, :cols], all_low[where, :cols] = halves(light[quad, row, at(piece)] + added[quad])
        accumulate(acc_z, piece * block, piece * block + block // 2, 0, False)

    gram_part[:cols] = acc_z[:, :cols]
    gram_part[cols:size] = acc_z[:, cols:size]
    gram_part[size : size + cols] = acc_n[:, :cols]
    if gram_part.shape[0] > size + cols:
        gram_part[size + cols :] = jnp.zeros((gram_part.shape[0] - size - cols, cols), jnp.float32)
    gram_steps = reduction(count, *gram_scratch)
    next(gram_steps)
    for part, (acc, begin) in enumerate(((acc_z, size), (acc_z, size + cols), (acc_n, cols), (acc_n, size))):
        cross_part[part * cols : (part + 1) * cols] = acc[:, begin : begin + cols]
    for piece in range(parts):
        sent(functools.partial(message, values, True, 0, 0, piece))
        sent(functools.partial(message, partial, False, 0, 1, piece))
    sent(rates)
    cross_steps = reduction(count, *cross_scratch)
    for step in range(1, 7):
        next(gram_steps, None)
        if step >= lag:
            next(cross_steps)

    row_ids = lax.broadcasted_iota(jnp.int32, (size, size), 0)
    col_ids = lax.broadcasted_iota(jnp.int32, (size, size), 1)
    work[:cols, :cols] = gram_full[:cols]
    work[:cols, cols:size] = gram_full[cols:size]
    work[cols:, :cols] = jnp.zeros((cols, cols), jnp.float32)
    work[cols:, cols:size] = gram_full[size : size + cols]
    work[:, size:] = (row_ids == col_ids).astype(jnp.float32)
    for start in range(0, size, tile):
        stop = start + tile
        small = tile_inverse(work[start:stop, start:stop])
        panel = mul(small, work[start:stop, :], (1, 0))
        work[start:stop, :] = panel
        if stop < size:
            base, end = stop // 128 * 128, size + (stop + 127) // 128 * 128
            update = mul(panel[:, base:size].T, panel[:, base:end], (1, 0))
            work[stop:, base:end] = work[stop:, base:end] - update[stop - base :]
        next(cross_steps, None)
    upper = jnp.where(row_ids <= col_ids, work[:, :size], 0.0)
    inverse = jnp.where(row_ids >= col_ids, work[:, size:], 0.0)
    bar = jnp.where(row_ids <= col_ids, rbar_ref[...], 0.0)
    cross = jnp.concatenate(
        [
            jnp.concatenate([cross_full[:cols], cross_full[cols:size]], axis=1),
            jnp.concatenate([cross_full[size : size + cols], cross_full[size + cols :]], axis=1),
        ],
        axis=0,
    )
    middle = mul(upper, bar, (1, 1)) - mul(cross.T, inverse, (1, 1))
    symmetric = jnp.where(row_ids >= col_ids, middle, middle.T)
    mix = mul(inverse.T, mul(symmetric, inverse, (1, 0)), (1, 0))
    for begin, value in ((0, mix), (size, inverse)):
        lines = slice(begin, begin + size)
        high, rest = halves(value)
        weight_z[lines, :cols], weight_z[lines, cols:] = high[:, :cols], rest[:, :cols]
        weight_n[lines, :cols], weight_n[lines, cols:] = high[:, cols:], rest[:, cols:]

    def gradient(weight, piece):
        lines = slice(piece * block, (piece + 1) * block)
        both = dot16(all_high[lines], weight[...], (1, 0))
        return both[:, :cols] + both[:, cols:] + dot16(all_low[lines], weight[:, :cols], (1, 0))

    for piece in range(parts):
        grad = gradient(weight_z, piece)
        for quad in range(quads):
            for row in range(rows):
                start = (quad * rows + row) * chunk
                values[quad, row, inner(piece)] = grad[start : start + chunk]
                if quad < 2:
                    hop[quad, row, inner(piece)] = coef(5, row, piece) * grad[start : start + chunk]
        send(functools.partial(message, hop, True, 1, 0, piece))
        if piece:
            first_term(1, hop, piece - 1)
    first_term(1, hop, parts - 1)
    for piece in range(parts):
        grad = gradient(weight_n, piece)
        for quad in range(quads):
            for row in range(rows):
                start = (quad * rows + row) * chunk
                noise_out[quad, row, at(piece)] = grad[start : start + chunk]

    def finish_back(piece):
        for row in range(rows):
            for quad, value in enumerate(second_term(1, row, piece)):
                z_out[quad, row, at(piece)] = value

    for piece in range(parts):
        first_halo(1, hop, piece)
        if piece:
            finish_back(piece - 1)
    finish_back(parts - 1)
    for piece in range(parts):
        for row, added in enumerate(last_halo(1, hop, piece)):
            for quad in range(2):
                z_out[quad, row, at(piece)] = z_out[quad, row, at(piece)] + added[quad]
    for piece in range(parts):
        sent(functools.partial(message, hop, True, 1, 0, piece))
        sent(functools.partial(message, partial, False, 1, 1, piece))


def on_device(cell_coeffs, z_factor, noise_cols, q_bar, r_bar):
    count = lax.axis_size("row")
    quads, rows, cells, cols = z_factor.shape
    size = 2 * cols
    total = quads * rows * cells
    unit = 8 * count
    gram_rows = (size + cols + unit - 1) // unit * unit
    padded = cells + 2 * margin
    plane = (cells, cols)
    here = pl.BlockSpec(memory_space=pltpu.VMEM)
    far = pl.BlockSpec(memory_space=pl.ANY)

    def floats(*shape):
        return pltpu.VMEM(shape, jnp.float32)

    def shorts(*shape):
        return pltpu.VMEM(shape, jnp.bfloat16)

    return pl.pallas_call(
        functools.partial(whole_kernel, count),
        out_shape=(
            jax.ShapeDtypeStruct(z_factor.shape, jnp.float32),
            jax.ShapeDtypeStruct(noise_cols.shape, jnp.float32),
        ),
        in_specs=[here, far, far, far, here],
        out_specs=(here, here),
        scratch_shapes=[
            floats(16, cells),
            floats(2, 8, cells),
            floats(6 * rows + 2, *plane),
            floats(quads, rows, padded, cols),
            floats(2, rows, padded, cols),
            floats(2, rows, padded, cols),
            floats(quads, rows, *plane),
            floats(2, rows, *plane),
            floats(2, rows, *plane),
            floats(2, 2, 4, *plane),
            floats(quads, rows, *plane),
            floats(quads, rows, cells, size),
            shorts(total, 2 * size),
            shorts(total, 2 * size),
            floats(cols, 2 * size),
            floats(cols, 2 * size - cols),
            floats(size, 2 * size),
            shorts(2 * size, size),
            shorts(2 * size, size),
            pltpu.SemaphoreType.DMA((3,)),
        ]
        + [pltpu.SemaphoreType.DMA((4 * parts + 1,))] * 4
        + reduction_scratch(count, gram_rows, cols)
        + reduction_scratch(count, 4 * cols, cols),
        compiler_params=pltpu.CompilerParams(
            collective_id=0, has_side_effects=True, vmem_limit_bytes=48 * 2**20
        ),
    )(cell_coeffs, z_factor, noise_cols, q_bar, r_bar)


def solution(mesh):
    return jax.shard_map(
        on_device,
        mesh=mesh,
        in_specs=(
            P(None, "row", None),
            P(None, ("grp", "row"), None, None),
            P(None, ("grp", "row"), None, None),
            P(None, ("grp", "row"), None, None),
            P("grp", None),
        ),
        out_specs=(P(None, ("grp", "row"), None, None), P(None, ("grp", "row"), None, None)),
        check_vma=False,
    )
```

time: 91.7 us -> 84.3 us (0.919)
  matrix products: 7.16 us -> 0 us
  local copies, waits for them, and re-layouts: 2.72 us -> 5.36 us
  Pallas kernels: 79.2 us -> 78.1 us
  other arithmetic: 0.95 us -> 0 us
    dot_general x1 -> x0, matrix products: 7.16 us -> none  [on_device(): lax.dot_general(both, flat_rows, (((0,), (0,)), ((), ())), precision=lax....]
    unnamed x9 -> x8, local copies, waits for them, and re-layouts: 2.57 us -> 5.36 us
    pallas_call x5 -> x1, Pallas kernels: 79.2 us -> 78.1 us  [on_device(): pl.pallas_call(functools.partial(whole_kernel, count), out_shape=(jax.Sha...]
    mul x1 -> x0, other arithmetic: 0.95 us -> none  [on_device(): scaled = cell_coeffs * jnp.array(rate_scales, jnp.float32)[:, None, None]]
where the time goes in v1:
time: 84.3 us; the launch traced here: 84.1 us
  Pallas kernels  78.1 us (93%)
  local copies, waits for them, and re-layouts  5.36 us (6%)
    pallas_call x1, Pallas kernels, on_device(): pl.pallas_call(functools.partial(whole_kernel, count), out_shape=(jax.Sha...  78.1 us
    unnamed x8, local copies, waits for them, and re-layouts  5.36 us

profile of v1, /device:TPU:9, one launch (start us, length us, event | category | flops | bytes accessed | tf_op | source)
XLA Modules:
  0.0 84.1 jit_solution(11190885260642477294)
XLA Ops:
  0.6 0.0 copy-start
  0.6 1.4 %copy-done = f32[4,2,384,128]{3,2,1,0:T(8,128)S(1)} copy-done((f32[4,2,384,128]{3,2,1,0:T(8,128)S(1)}, f32[4,2,384,128]{3,2,1,0:T(8,128)}, u32[]{:S(2)}) %copy-start) | copy-done | bytes 1572888
  2.0 0.0 copy-start.1
  2.0 0.9 %copy-done.1 = f32[256,256]{1,0:T(8,128)S(1)} copy-done((f32[256,256]{1,0:T(8,128)S(1)}, f32[256,256]{1,0:T(8,128)}, u32[]{:S(2)}) %copy-start.1) | copy-done | bytes 262168
  3.0 0.0 copy-start.2
  3.0 0.7 copy-done.2
  3.7 78.1 %shard_map.68 = (f32[4,2,384,128]{3,2,1,0:T(8,128)S(1)}, f32[4,2,384,128]{3,2,1,0:T(8,128)S(1)}) custom-call(f32[6,2,384]{2,1,0:T(2,128)S(1)} %copy-done.2, f32[4,2,384,128]{3,2,1,0:T(8,128)S(1)} %copy-done, f32[4,2,384,128]{3,2,1,0:T(8,128)} %noise_hbm.1, f32[4,2,384,256]{3,2,1,0:T(8,128)} %bar_hbm.1, f32[256,256]{1,0:T(8,128)S(1)} %copy-done.1), custom_call_target="tpu_custom_call" | custom-call | tf_op jit(solution)/shard_map/pallas_call | solution.py:520
  81.8 1.1 %copy.9 = f32[4,2,384,128]{3,2,1,0:T(8,128)} copy(f32[4,2,384,128]{3,2,1,0:T(8,128)S(1)} %get-tuple-element.4) | data formatting | bytes 3145728
  82.9 1.1 %copy.10 = f32[4,2,384,128]{3,2,1,0:T(8,128)} copy(f32[4,2,384,128]{3,2,1,0:T(8,128)S(1)} %get-tuple-element.5) | data formatting | bytes 3145728
Async XLA Ops:
  0.6 1.4 %copy-start = (f32[4,2,384,128]{3,2,1,0:T(8,128)S(1)}, f32[4,2,384,128]{3,2,1,0:T(8,128)}, u32[]{:S(2)}) copy-start(f32[4,2,384,128]{3,2,1,0:T(8,128)} %z_hbm.1) | copy-start | bytes 4718596
  2.0 0.9 %copy-start.1 = (f32[256,256]{1,0:T(8,128)S(1)}, f32[256,256]{1,0:T(8,128)}, u32[]{:S(2)}) copy-start(f32[256,256]{1,0:T(8,128)} %rbar_ref.1) | copy-start | bytes 786436
  3.0 0.7 copy-start.2

commit v2 on v1

--- a/solution.py
+++ b/solution.py
@@ -13,21 +13,19 @@
 
 parts = 6
 margin = 8
-lag = 2
 tile = 32
 
 
-def reduction(count, part_ref, half_in, half_sum, quarter_in, quarter_sum, piece_in, full, send_sem, recv_sem, peer_send, peer_recv, back_send, back_recv):
+def reduction(count, part_ref, half_in, half_sum, piece_in, full, pair_send, pair_recv, peer_send, peer_recv, back_send, back_recv):
     rows = part_ref.shape[0]
-    peers = count // 4
-    half, quarter, piece = rows // 2, rows // 4, rows // count
+    chips = count // 2
+    half, piece = rows // 2, rows // count
     me = lax.axis_index("row")
-    low, mid, top = lax.rem(me, 2), lax.rem(me // 2, 2), me // 4
+    low, chip = lax.rem(me, 2), me // 2
     pair = me + 1 - 2 * low
-    across = me + 2 - 4 * mid
 
     def other(step):
-        return lax.rem(top + step, peers)
+        return lax.rem(chip + step, chips)
 
     def copy_to(source, target, sends, recvs, slot, where):
         return pltpu.make_async_remote_copy(
@@ -40,74 +38,59 @@
         )
 
     first = copy_to(
-        part_ref.at[pl.ds(pl.multiple_of((1 - low) * half, 8), half)], half_in, send_sem, recv_sem, 0, pair
+        part_ref.at[pl.ds(pl.multiple_of((1 - low) * half, 8), half)], half_in, pair_send, pair_recv, 0, pair
     )
     first.start()
     yield
     first.wait()
     half_sum[...] = part_ref[pl.ds(pl.multiple_of(low * half, 8), half)] + half_in[...]
-    second = copy_to(
-        half_sum.at[pl.ds(pl.multiple_of((1 - mid) * quarter, 8), quarter)], quarter_in, send_sem, recv_sem, 1, across
-    )
-    second.start()
-    yield
-    second.wait()
-    quarter_sum[...] = half_sum[pl.ds(pl.multiple_of(mid * quarter, 8), quarter)] + quarter_in[...]
     outgoing = [
         copy_to(
-            quarter_sum.at[pl.ds(pl.multiple_of(other(step) * piece, 8), piece)],
+            half_sum.at[pl.ds(pl.multiple_of(other(step) * piece, 8), piece)],
             piece_in.at[step],
             peer_send,
             peer_recv,
             step,
-            other(step) * 4 + lax.rem(me, 4),
+            other(step) * 2 + low,
         )
-        for step in range(1, peers)
+        for step in range(1, chips)
     ]
     for copy in outgoing:
         copy.start()
     yield
-    total = quarter_sum[pl.ds(pl.multiple_of(top * piece, 8), piece)]
+    total = half_sum[pl.ds(pl.multiple_of(chip * piece, 8), piece)]
     for step, copy in enumerate(outgoing, 1):
         copy.wait()
         total = total + piece_in[step]
-    base = low * half + mid * quarter
-    mine = pl.ds(pl.multiple_of(base + top * piece, 8), piece)
+    mine = pl.ds(pl.multiple_of(low * half + chip * piece, 8), piece)
     full[mine] = total
     returning = [
-        copy_to(full.at[mine], full.at[mine], back_send, back_recv, step, other(step) * 4 + lax.rem(me, 4))
-        for step in range(1, peers)
+        copy_to(full.at[mine], full.at[mine], back_send, back_recv, step, other(step) * 2 + low)
+        for step in range(1, chips)
     ]
     for copy in returning:
         copy.start()
     yield
     for copy in returning:
         copy.wait()
-    own_quarter = full.at[pl.ds(pl.multiple_of(base, 8), quarter)]
-    third = copy_to(own_quarter, own_quarter, send_sem, recv_sem, 2, across)
-    third.start()
+    own_half = full.at[pl.ds(pl.multiple_of(low * half, 8), half)]
+    last = copy_to(own_half, own_half, pair_send, pair_recv, 1, pair)
+    last.start()
     yield
-    third.wait()
-    own_half = full.at[pl.ds(pl.multiple_of(low * half, 8), half)]
-    fourth = copy_to(own_half, own_half, send_sem, recv_sem, 3, pair)
-    fourth.start()
-    yield
-    fourth.wait()
+    last.wait()
 
 
 def reduction_scratch(count, rows, cols):
-    peers = count // 4
+    chips = count // 2
     return [
         pltpu.VMEM((rows, cols), jnp.float32),
         pltpu.VMEM((rows // 2, cols), jnp.float32),
         pltpu.VMEM((rows // 2, cols), jnp.float32),
-        pltpu.VMEM((rows // 4, cols), jnp.float32),
-        pltpu.VMEM((rows // 4, cols), jnp.float32),
-        pltpu.VMEM((peers, rows // count, cols), jnp.float32),
+        pltpu.VMEM((chips, rows // count, cols), jnp.float32),
         pltpu.VMEM((rows, cols), jnp.float32),
-        pltpu.SemaphoreType.DMA((4,)),
-        pltpu.SemaphoreType.DMA((4,)),
-    ] + [pltpu.SemaphoreType.DMA((peers,))] * 4
+        pltpu.SemaphoreType.DMA((2,)),
+        pltpu.SemaphoreType.DMA((2,)),
+    ] + [pltpu.SemaphoreType.DMA((chips,))] * 4
 
 
 def tile_inverse(block):
@@ -155,7 +138,7 @@
 def whole_kernel(
     count, coef_ref, z_hbm, noise_hbm, bar_hbm, rbar_ref, z_out, noise_out,
     coef_rows, halo_rows, coefs, values, hop, second, first, partial, light, halo,
-    noise_in, bar_in, all_high, all_low, acc_z, acc_n, work, weight_z, weight_n,
+    noise_in, bar_in, result, all_high, all_low, acc_z, acc_n, work, weight_z, weight_n,
     load_sem, send_low, recv_low, send_high, recv_high, *sums,
 ):
     quads, rows, cells, cols = z_hbm.shape
@@ -165,9 +148,9 @@
     block = strips * chunk
     me = lax.axis_index("row")
     has_low, has_high = me > 0, me < count - 1
-    gram_scratch, cross_scratch = sums[:13], sums[13:]
-    gram_part, gram_full = gram_scratch[0], gram_scratch[6]
-    cross_part, cross_full = cross_scratch[0], cross_scratch[6]
+    gram_scratch, cross_scratch = sums[:11], sums[11:]
+    gram_part, gram_full = gram_scratch[0], gram_scratch[4]
+    cross_part, cross_full = cross_scratch[0], cross_scratch[4]
 
     load_z = pltpu.make_async_copy(z_hbm, values.at[:, :, margin : margin + cells], load_sem.at[0])
     load_noise = pltpu.make_async_copy(noise_hbm, noise_in, load_sem.at[1])
@@ -175,10 +158,9 @@
     load_z.start()
 
     barrier = pltpu.get_barrier_semaphore()
-    peers = count // 4
-    low, mid, top = lax.rem(me, 2), lax.rem(me // 2, 2), me // 4
-    friends = [me + 1 - 2 * low, me + 2 - 4 * mid]
-    friends += [lax.rem(top + step, peers) * 4 + lax.rem(me, 4) for step in range(1, peers)]
+    low, chip = lax.rem(me, 2), me // 2
+    friends = [me + 1 - 2 * low]
+    friends += [lax.rem(chip + step, count // 2) * 2 + low for step in range(1, count // 2)]
 
     @pl.when(has_low)
     def _():
@@ -407,18 +389,20 @@
     if gram_part.shape[0] > size + cols:
         gram_part[size + cols :] = jnp.zeros((gram_part.shape[0] - size - cols, cols), jnp.float32)
     gram_steps = reduction(count, *gram_scratch)
+    cross_steps = reduction(count, *cross_scratch)
     next(gram_steps)
     for part, (acc, begin) in enumerate(((acc_z, size), (acc_z, size + cols), (acc_n, cols), (acc_n, size))):
         cross_part[part * cols : (part + 1) * cols] = acc[:, begin : begin + cols]
+    next(cross_steps)
+    next(gram_steps)
     for piece in range(parts):
         sent(functools.partial(message, values, True, 0, 0, piece))
         sent(functools.partial(message, partial, False, 0, 1, piece))
     sent(rates)
-    cross_steps = reduction(count, *cross_scratch)
-    for step in range(1, 7):
-        next(gram_steps, None)
-        if step >= lag:
-            next(cross_steps)
+    next(gram_steps)
+    next(cross_steps)
+    next(gram_steps)
+    next(gram_steps, None)
 
     row_ids = lax.broadcasted_iota(jnp.int32, (size, size), 0)
     col_ids = lax.broadcasted_iota(jnp.int32, (size, size), 1)
@@ -436,7 +420,8 @@
             base, end = stop // 128 * 128, size + (stop + 127) // 128 * 128
             update = mul(panel[:, base:size].T, panel[:, base:end], (1, 0))
             work[stop:, base:end] = work[stop:, base:end] - update[stop - base :]
-        next(cross_steps, None)
+        if start // tile in (2, 5, 7):
+            next(cross_steps, None)
     upper = jnp.where(row_ids <= col_ids, work[:, :size], 0.0)
     inverse = jnp.where(row_ids >= col_ids, work[:, size:], 0.0)
     bar = jnp.where(row_ids <= col_ids, rbar_ref[...], 0.0)
@@ -478,22 +463,30 @@
         for quad in range(quads):
             for row in range(rows):
                 start = (quad * rows + row) * chunk
-                noise_out[quad, row, at(piece)] = grad[start : start + chunk]
+                noise_in[quad, row, at(piece)] = grad[start : start + chunk]
+    store_noise = pltpu.make_async_copy(noise_in, noise_out, load_sem.at[1])
+    store_noise.start()
 
     def finish_back(piece):
         for row in range(rows):
             for quad, value in enumerate(second_term(1, row, piece)):
-                z_out[quad, row, at(piece)] = value
+                result[quad, row, at(piece)] = value
 
     for piece in range(parts):
         first_halo(1, hop, piece)
         if piece:
             finish_back(piece - 1)
     finish_back(parts - 1)
+    stores = [store_noise, pltpu.make_async_copy(result.at[2:4], z_out.at[2:4], load_sem.at[0])]
+    stores[1].start()
     for piece in range(parts):
         for row, added in enumerate(last_halo(1, hop, piece)):
             for quad in range(2):
-                z_out[quad, row, at(piece)] = z_out[quad, row, at(piece)] + added[quad]
+                result[quad, row, at(piece)] = result[quad, row, at(piece)] + added[quad]
+        stores.append(pltpu.make_async_copy(result.at[0:2, :, at(piece)], z_out.at[0:2, :, at(piece)], load_sem.at[3 + piece]))
+        stores[-1].start()
+    for store in stores:
+        store.wait()
     for piece in range(parts):
         sent(functools.partial(message, hop, True, 1, 0, piece))
         sent(functools.partial(message, partial, False, 1, 1, piece))
@@ -524,7 +517,7 @@
             jax.ShapeDtypeStruct(noise_cols.shape, jnp.float32),
         ),
         in_specs=[here, far, far, far, here],
-        out_specs=(here, here),
+        out_specs=(far, far),
         scratch_shapes=[
             floats(16, cells),
             floats(2, 8, cells),
@@ -538,6 +531,7 @@
             floats(2, 2, 4, *plane),
             floats(quads, rows, *plane),
             floats(quads, rows, cells, size),
+            floats(quads, rows, *plane),
             shorts(total, 2 * size),
             shorts(total, 2 * size),
             floats(cols, 2 * size),
@@ -545,13 +539,13 @@
             floats(size, 2 * size),
             shorts(2 * size, size),
             shorts(2 * size, size),
-            pltpu.SemaphoreType.DMA((3,)),
+            pltpu.SemaphoreType.DMA((3 + parts,)),
         ]
         + [pltpu.SemaphoreType.DMA((4 * parts + 1,))] * 4
         + reduction_scratch(count, gram_rows, cols)
         + reduction_scratch(count, 4 * cols, cols),
         compiler_params=pltpu.CompilerParams(
-            collective_id=0, has_side_effects=True, vmem_limit_bytes=48 * 2**20
+            collective_id=0, has_side_effects=True, vmem_limit_bytes=62 * 2**20
         ),
     )(cell_coeffs, z_factor, noise_cols, q_bar, r_bar)
 

time: 84.3 us -> 80.5 us (0.955)
  Pallas kernels: 78.1 us -> 75.7 us
  local copies, waits for them, and re-layouts: 5.36 us -> 3.93 us
    pallas_call x1, Pallas kernels: 78.1 us -> 75.7 us  [on_device(): pl.pallas_call(functools.partial(whole_kernel, count), out_shape=(jax.Sha...]
    unnamed x8 -> x4, local copies, waits for them, and re-layouts: 5.36 us -> 3.93 us
where the time goes in v2:
time: 80.5 us; the launch traced here: 80.3 us
  Pallas kernels  75.7 us (94%)
  local copies, waits for them, and re-layouts  3.93 us (5%)
    pallas_call x1, Pallas kernels, on_device(): pl.pallas_call(functools.partial(whole_kernel, count), out_shape=(jax.Sha...  75.7 us
    unnamed x4, local copies, waits for them, and re-layouts  3.93 us

profile of v2, /device:TPU:9, one launch (start us, length us, event | category | flops | bytes accessed | tf_op | source)
XLA Modules:
  0.0 80.3 jit_solution(3571119378954585536)
XLA Ops:
  0.6 75.7 %shard_map.68 = (f32[4,2,384,128]{3,2,1,0:T(8,128)}, f32[4,2,384,128]{3,2,1,0:T(8,128)}) custom-call(f32[6,2,384]{2,1,0:T(2,128)} %coef_ref.1, f32[4,2,384,128]{3,2,1,0:T(8,128)} %z_hbm.1, f32[4,2,384,128]{3,2,1,0:T(8,128)} %noise_hbm.1, f32[4,2,384,256]{3,2,1,0:T(8,128)} %bar_hbm.1, f32[256,256]{1,0:T(8,128)} %rbar_ref.1), custom_call_target="tpu_custom_call" | custom-call | tf_op jit(solution)/shard_map/pallas_call | solution.py:513
  76.4 0.0 copy-start
  76.4 2.8 %copy.9 = f32[4,2,384,128]{3,2,1,0:T(8,128)} copy(f32[4,2,384,128]{3,2,1,0:T(8,128)} %get-tuple-element.4) | data formatting | bytes 3145728
  79.2 0.0 copy-done
  79.2 1.1 %copy.10 = f32[4,2,384,128]{3,2,1,0:T(8,128)} copy(f32[4,2,384,128]{3,2,1,0:T(8,128)S(1)} %copy-done) | data formatting | bytes 3145728
Async XLA Ops:
  76.4 2.8 %copy-start = (f32[4,2,384,128]{3,2,1,0:T(8,128)S(1)}, f32[4,2,384,128]{3,2,1,0:T(8,128)}, u32[]{:S(2)}) copy-start(f32[4,2,384,128]{3,2,1,0:T(8,128)} %get-tuple-element.5) | copy-start | bytes 4718596

commit v3 on v2

--- a/solution.py
+++ b/solution.py
@@ -130,13 +130,29 @@
     return lax.dot_general(a, b, ((contract[0:1], contract[1:2]), ((), ())), preferred_element_type=jnp.float32)
 
 
+def thirds(value):
+    high = value.astype(jnp.bfloat16)
+    value = value - high.astype(jnp.float32)
+    mid = value.astype(jnp.bfloat16)
+    return high, mid, (value - mid.astype(jnp.float32)).astype(jnp.bfloat16)
+
+
+def packed(left, right):
+    lh, lm, ll = thirds(left)
+    rh, rm, rl = thirds(right)
+    return dot16(
+        jnp.concatenate([lh, lh, lm, lm, lh, ll], axis=0), jnp.concatenate([rh, rm, rh, rm, rl, rh], axis=0), (0, 0)
+    )
+
+
 def halves(value):
     high = value.astype(jnp.bfloat16)
     return high, (value - high.astype(jnp.float32)).astype(jnp.bfloat16)
 
 
 def whole_kernel(
-    count, coef_ref, z_hbm, noise_hbm, bar_hbm, rbar_ref, z_out, noise_out,
+    count, coef_hbm, z_hbm, noise_hbm, bar_hbm, rbar_hbm, z_out, noise_out,
+    coef_ref, rbar_ref,
     coef_rows, halo_rows, coefs, values, hop, second, first, partial, light, halo,
     noise_in, bar_in, result, all_high, all_low, acc_z, acc_n, work, weight_z, weight_n,
     load_sem, send_low, recv_low, send_high, recv_high, *sums,
@@ -155,6 +171,9 @@
     load_z = pltpu.make_async_copy(z_hbm, values.at[:, :, margin : margin + cells], load_sem.at[0])
     load_noise = pltpu.make_async_copy(noise_hbm, noise_in, load_sem.at[1])
     load_bar = pltpu.make_async_copy(bar_hbm, bar_in, load_sem.at[2])
+    load_coef = pltpu.make_async_copy(coef_hbm, coef_ref, load_sem.at[3])
+    load_rbar = pltpu.make_async_copy(rbar_hbm, rbar_ref, load_sem.at[4])
+    load_coef.start()
     load_z.start()
 
     barrier = pltpu.get_barrier_semaphore()
@@ -174,6 +193,7 @@
         pl.semaphore_signal(barrier, inc=1, device_id={"row": friend}, device_id_type=pl.DeviceIdType.MESH)
     load_noise.start()
     load_bar.start()
+    load_rbar.start()
 
     def link(source, target, slot, upward):
         sends, recvs = (send_high, recv_high) if upward else (send_low, recv_low)
@@ -238,6 +258,7 @@
         start = piece * block + (quad * rows + row) * chunk
         return slice(start, start + chunk)
 
+    load_coef.wait()
     for kind in range(6):
         for row in range(rows):
             line = coef_ref[kind, row : row + 1] * jnp.float32(rate_scales[kind])
@@ -402,6 +423,7 @@
     next(gram_steps)
     next(cross_steps)
     next(gram_steps)
+    next(cross_steps)
     next(gram_steps, None)
 
     row_ids = lax.broadcasted_iota(jnp.int32, (size, size), 0)
@@ -414,16 +436,17 @@
     for start in range(0, size, tile):
         stop = start + tile
         small = tile_inverse(work[start:stop, start:stop])
-        panel = mul(small, work[start:stop, :], (1, 0))
+        panel = packed(small.T, work[start:stop, :])
         work[start:stop, :] = panel
         if stop < size:
             base, end = stop // 128 * 128, size + (stop + 127) // 128 * 128
-            update = mul(panel[:, base:size].T, panel[:, base:end], (1, 0))
+            update = packed(panel[:, base:size], panel[:, base:end])
             work[stop:, base:end] = work[stop:, base:end] - update[stop - base :]
-        if start // tile in (2, 5, 7):
+        if start // tile in (4, 7):
             next(cross_steps, None)
     upper = jnp.where(row_ids <= col_ids, work[:, :size], 0.0)
     inverse = jnp.where(row_ids >= col_ids, work[:, size:], 0.0)
+    load_rbar.wait()
     bar = jnp.where(row_ids <= col_ids, rbar_ref[...], 0.0)
     cross = jnp.concatenate(
         [
@@ -483,7 +506,7 @@
         for row, added in enumerate(last_halo(1, hop, piece)):
             for quad in range(2):
                 result[quad, row, at(piece)] = result[quad, row, at(piece)] + added[quad]
-        stores.append(pltpu.make_async_copy(result.at[0:2, :, at(piece)], z_out.at[0:2, :, at(piece)], load_sem.at[3 + piece]))
+        stores.append(pltpu.make_async_copy(result.at[0:2, :, at(piece)], z_out.at[0:2, :, at(piece)], load_sem.at[5 + piece]))
         stores[-1].start()
     for store in stores:
         store.wait()
@@ -501,7 +524,6 @@
     gram_rows = (size + cols + unit - 1) // unit * unit
     padded = cells + 2 * margin
     plane = (cells, cols)
-    here = pl.BlockSpec(memory_space=pltpu.VMEM)
     far = pl.BlockSpec(memory_space=pl.ANY)
 
     def floats(*shape):
@@ -516,9 +538,11 @@
             jax.ShapeDtypeStruct(z_factor.shape, jnp.float32),
             jax.ShapeDtypeStruct(noise_cols.shape, jnp.float32),
         ),
-        in_specs=[here, far, far, far, here],
+        in_specs=[far] * 5,
         out_specs=(far, far),
         scratch_shapes=[
+            floats(*cell_coeffs.shape),
+            floats(*r_bar.shape),
             floats(16, cells),
             floats(2, 8, cells),
             floats(6 * rows + 2, *plane),
@@ -539,7 +563,7 @@
             floats(size, 2 * size),
             shorts(2 * size, size),
             shorts(2 * size, size),
-            pltpu.SemaphoreType.DMA((3 + parts,)),
+            pltpu.SemaphoreType.DMA((5 + parts,)),
         ]
         + [pltpu.SemaphoreType.DMA((4 * parts + 1,))] * 4
         + reduction_scratch(count, gram_rows, cols)

time: 80.5 us -> 73.9 us (0.918)
  Pallas kernels: 75.7 us -> 69.1 us
    pallas_call x1, Pallas kernels: 75.7 us -> 69.1 us  [on_device(): pl.pallas_call(functools.partial(whole_kernel, count), out_shape=(jax.Sha...]
where the time goes in v3:
time: 73.9 us; the launch traced here: 73.7 us
  Pallas kernels  69.1 us (94%)
  local copies, waits for them, and re-layouts  3.93 us (5%)
    pallas_call x1, Pallas kernels, on_device(): pl.pallas_call(functools.partial(whole_kernel, count), out_shape=(jax.Sha...  69.1 us
    unnamed x4, local copies, waits for them, and re-layouts  3.93 us

profile of v3, /device:TPU:9, one launch (start us, length us, event | category | flops | bytes accessed | tf_op | source)
XLA Modules:
  0.0 73.7 jit_solution(11662855372339738788)
XLA Ops:
  0.6 69.1 %shard_map.68 = (f32[4,2,384,128]{3,2,1,0:T(8,128)}, f32[4,2,384,128]{3,2,1,0:T(8,128)}) custom-call(f32[6,2,384]{2,1,0:T(2,128)} %coef_hbm.1, f32[4,2,384,128]{3,2,1,0:T(8,128)} %z_hbm.1, f32[4,2,384,128]{3,2,1,0:T(8,128)} %noise_hbm.1, f32[4,2,384,256]{3,2,1,0:T(8,128)} %bar_hbm.1, f32[256,256]{1,0:T(8,128)} %rbar_hbm.1), custom_call_target="tpu_custom_call" | custom-call | tf_op jit(solution)/shard_map/pallas_call | solution.py:535
  69.8 0.0 copy-start
  69.8 2.8 %copy.9 = f32[4,2,384,128]{3,2,1,0:T(8,128)} copy(f32[4,2,384,128]{3,2,1,0:T(8,128)} %get-tuple-element.4) | data formatting | bytes 3145728
  72.6 0.0 copy-done
  72.6 1.1 %copy.10 = f32[4,2,384,128]{3,2,1,0:T(8,128)} copy(f32[4,2,384,128]{3,2,1,0:T(8,128)S(1)} %copy-done) | data formatting | bytes 3145728
Async XLA Ops:
  69.8 2.8 %copy-start = (f32[4,2,384,128]{3,2,1,0:T(8,128)S(1)}, f32[4,2,384,128]{3,2,1,0:T(8,128)}, u32[]{:S(2)}) copy-start(f32[4,2,384,128]{3,2,1,0:T(8,128)} %get-tuple-element.5) | copy-start | bytes 4718596

commit v4 on v3

--- a/solution.py
+++ b/solution.py
@@ -12,6 +12,7 @@
 exact = lax.Precision.HIGHEST
 
 parts = 6
+early = (2,)
 margin = 8
 tile = 32
 
@@ -152,7 +153,7 @@
 
 def whole_kernel(
     count, coef_hbm, z_hbm, noise_hbm, bar_hbm, rbar_hbm, z_out, noise_out,
-    coef_ref, rbar_ref,
+    coef_ref, rbar_ref, ahead_out, ahead_in,
     coef_rows, halo_rows, coefs, values, hop, second, first, partial, light, halo,
     noise_in, bar_in, result, all_high, all_low, acc_z, acc_n, work, weight_z, weight_n,
     load_sem, send_low, recv_low, send_high, recv_high, *sums,
@@ -217,6 +218,11 @@
 
     def rates(upward):
         return link(coef_rows.at[8:16], halo_rows.at[0 if upward else 1], 4 * parts, upward)
+
+    def ahead(slot, upward):
+        return link(
+            ahead_out.at[1 if upward else 0, slot], ahead_in.at[0 if upward else 1, slot], 4 * parts + 1 + slot, upward
+        )
 
     def send(copy_of):
         @pl.when(has_high)
@@ -312,10 +318,12 @@
                 first[quad, row, at(piece)] = value
                 if quad < 2:
                     partial[quad, row, at(piece)] = coef(5, row, piece) * value if run else value
-        send(functools.partial(message, partial, False, run, 1, piece))
+        if run == 0 or piece not in early:
+            send(functools.partial(message, partial, False, run, 1, piece))
 
     def first_halo(run, source, piece):
-        receive(functools.partial(message, source, True, run, 0, piece))
+        if run == 0 or piece not in early:
+            receive(functools.partial(message, source, True, run, 0, piece))
         for row in range(rows):
             halo_x, halo_p = halo[run, row, 0, at(piece)], halo[run, row, 1, at(piece)]
             hopping = coef(5, row, piece)
@@ -334,7 +342,8 @@
         return [value_at(quad, row, piece) + first_at(quad, row, piece) + 0.5 * found[quad] for quad in range(4)]
 
     def last_halo(run, source, piece):
-        receive(functools.partial(message, partial, False, run, 1, piece))
+        if run == 0 or piece not in early:
+            receive(functools.partial(message, partial, False, run, 1, piece))
         found = []
         for row in range(rows):
             beyond = coefs[6 * rows + row, at(piece)]
@@ -390,6 +399,8 @@
             for quad in range(2, 4):
                 where = strip(piece, quad, row)
                 all_high[where, :cols], all_low[where, :cols] = halves(found[quad])
+            if piece in early:
+                first[3, row, at(piece)] = found[3]
         accumulate(acc_z, piece * block + block // 2, (piece + 1) * block, 0, piece == 0)
 
     for piece in range(parts):
@@ -401,8 +412,40 @@
         for row, added in enumerate(last_halo(0, values, piece)):
             for quad in range(2):
                 where = strip(piece, quad, row)
-                all_high[where, :cols], all_low[where, :cols] = halves(light[quad, row, at(piece)] + added[quad])
+                light[quad, row, at(piece)] = light[quad, row, at(piece)] + added[quad]
+                all_high[where, :cols], all_low[where, :cols] = halves(light[quad, row, at(piece)])
         accumulate(acc_z, piece * block, piece * block + block // 2, 0, False)
+
+    def fill_ahead():
+        for slot, piece in enumerate(early):
+            for row in range(rows):
+                for part in range(4):
+
+                    def get(quad, line, shift=0):
+                        where = slice(piece * chunk + shift, (piece + 1) * chunk + shift)
+                        if part == 0:
+                            return first[3, line, where] if quad == 3 else light[quad, line, where]
+                        if part == 1:
+                            return noise_in[quad, line, where]
+                        return bar_in[quad, line, where, (part - 2) * cols : (part - 1) * cols]
+
+                    def hop_rate(shift):
+                        return coefs[5 * rows + row, piece * chunk + shift : (piece + 1) * chunk + shift]
+
+                    xa, pa, pb = get(0, row), get(1, row), get(3, row)
+                    hops = [
+                        hop_rate(-1) * get(quad, row, -1)
+                        + hop_rate(1) * get(quad, row, 1)
+                        + coef(5, 1 - row, piece) * get(quad, 1 - row)
+                        for quad in range(2)
+                    ]
+                    detuning, coupling, cavity = [coef(kind, row, piece) for kind in (0, 2, 3)]
+                    found_x = detuning * pa - cavity * xa - coupling * pb + hops[1]
+                    found_p = -detuning * xa - cavity * pa - hops[0]
+                    for plane, value in enumerate((xa, pa, found_x, found_p)):
+                        ahead_out[row, slot, plane * chunk : (plane + 1) * chunk, part * cols : (part + 1) * cols] = (
+                            hop_rate(0) * value
+                        )
 
     gram_part[:cols] = acc_z[:, :cols]
     gram_part[cols:size] = acc_z[:, cols:size]
@@ -416,6 +459,7 @@
         cross_part[part * cols : (part + 1) * cols] = acc[:, begin : begin + cols]
     next(cross_steps)
     next(gram_steps)
+    fill_ahead()
     for piece in range(parts):
         sent(functools.partial(message, values, True, 0, 0, piece))
         sent(functools.partial(message, partial, False, 0, 1, piece))
@@ -425,6 +469,8 @@
     next(gram_steps)
     next(cross_steps)
     next(gram_steps, None)
+    for slot in range(len(early)):
+        send(functools.partial(ahead, slot))
 
     row_ids = lax.broadcasted_iota(jnp.int32, (size, size), 0)
     col_ids = lax.broadcasted_iota(jnp.int32, (size, size), 1)
@@ -477,10 +523,23 @@
                 values[quad, row, inner(piece)] = grad[start : start + chunk]
                 if quad < 2:
                     hop[quad, row, inner(piece)] = coef(5, row, piece) * grad[start : start + chunk]
-        send(functools.partial(message, hop, True, 1, 0, piece))
+        if piece not in early:
+            send(functools.partial(message, hop, True, 1, 0, piece))
         if piece:
             first_term(1, hop, piece - 1)
     first_term(1, hop, parts - 1)
+    for slot, piece in enumerate(early):
+        for side, has in enumerate((has_low, has_high)):
+
+            @pl.when(has)
+            def _():
+                ahead(slot, side == 0).wait_recv()
+                high, rest = halves(ahead_in[side, slot])
+                both = dot16(high, weight_z[...], (1, 0))
+                edge = both[:, :cols] + both[:, cols:] + dot16(rest, weight_z[:, :cols], (1, 0))
+                for plane in range(4):
+                    halo[1, side, plane, at(piece)] = edge[plane * chunk : (plane + 1) * chunk]
+
     for piece in range(parts):
         grad = gradient(weight_n, piece)
         for quad in range(quads):
@@ -510,9 +569,12 @@
         stores[-1].start()
     for store in stores:
         store.wait()
-    for piece in range(parts):
-        sent(functools.partial(message, hop, True, 1, 0, piece))
-        sent(functools.partial(message, partial, False, 1, 1, piece))
+    for slot in range(len(early)):
+        sent(functools.partial(ahead, slot))
+    for piece in range(parts):
+        if piece not in early:
+            sent(functools.partial(message, hop, True, 1, 0, piece))
+            sent(functools.partial(message, partial, False, 1, 1, piece))
 
 
 def on_device(cell_coeffs, z_factor, noise_cols, q_bar, r_bar):
@@ -543,6 +605,8 @@
         scratch_shapes=[
             floats(*cell_coeffs.shape),
             floats(*r_bar.shape),
+            floats(2, len(early), 4 * (cells // parts), 2 * size),
+            floats(2, len(early), 4 * (cells // parts), 2 * size),
             floats(16, cells),
             floats(2, 8, cells),
             floats(6 * rows + 2, *plane),
@@ -565,7 +629,7 @@
             shorts(2 * size, size),
             pltpu.SemaphoreType.DMA((5 + parts,)),
         ]
-        + [pltpu.SemaphoreType.DMA((4 * parts + 1,))] * 4
+        + [pltpu.SemaphoreType.DMA((4 * parts + 1 + len(early),))] * 4
         + reduction_scratch(count, gram_rows, cols)
         + reduction_scratch(count, 4 * cols, cols),
         compiler_params=pltpu.CompilerParams(

time: 73.9 us -> 71.1 us (0.962)
  Pallas kernels: 69.1 us -> 66.4 us
    pallas_call x1, Pallas kernels: 69.1 us -> 66.4 us  [on_device(): pl.pallas_call(functools.partial(whole_kernel, count), out_shape=(jax.Sha...]
where the time goes in v4:
time: 71.1 us; the launch traced here: 70.9 us
  Pallas kernels  66.4 us (93%)
  local copies, waits for them, and re-layouts  3.93 us (6%)
    pallas_call x1, Pallas kernels, on_device(): pl.pallas_call(functools.partial(whole_kernel, count), out_shape=(jax.Sha...  66.4 us
    unnamed x4, local copies, waits for them, and re-layouts  3.93 us

profile of v4, /device:TPU:9, one launch (start us, length us, event | category | flops | bytes accessed | tf_op | source)
XLA Modules:
  0.0 70.9 jit_solution(18186677721286476023)
XLA Ops:
  0.6 66.4 %shard_map.68 = (f32[4,2,384,128]{3,2,1,0:T(8,128)}, f32[4,2,384,128]{3,2,1,0:T(8,128)}) custom-call(f32[6,2,384]{2,1,0:T(2,128)} %coef_hbm.1, f32[4,2,384,128]{3,2,1,0:T(8,128)} %z_hbm.1, f32[4,2,384,128]{3,2,1,0:T(8,128)} %noise_hbm.1, f32[4,2,384,256]{3,2,1,0:T(8,128)} %bar_hbm.1, f32[256,256]{1,0:T(8,128)} %rbar_hbm.1), custom_call_target="tpu_custom_call" | custom-call | tf_op jit(solution)/shard_map/pallas_call | solution.py:597
  67.0 0.0 copy-start
  67.0 2.8 %copy.9 = f32[4,2,384,128]{3,2,1,0:T(8,128)} copy(f32[4,2,384,128]{3,2,1,0:T(8,128)} %get-tuple-element.4) | data formatting | bytes 3145728
  69.8 0.0 copy-done
  69.8 1.1 %copy.10 = f32[4,2,384,128]{3,2,1,0:T(8,128)} copy(f32[4,2,384,128]{3,2,1,0:T(8,128)S(1)} %copy-done) | data formatting | bytes 3145728
Async XLA Ops:
  67.0 2.8 %copy-start = (f32[4,2,384,128]{3,2,1,0:T(8,128)S(1)}, f32[4,2,384,128]{3,2,1,0:T(8,128)}, u32[]{:S(2)}) copy-start(f32[4,2,384,128]{3,2,1,0:T(8,128)} %get-tuple-element.5) | copy-start | bytes 4718596

commit v5 on v4

--- a/solution.py
+++ b/solution.py
@@ -9,7 +9,6 @@
 
 rate_scales = (0.4, 0.4, 0.1, 0.2, 0.1, 0.1)
 extra_scales = (1.0, 1.0, 2.0, 0.5, 0.5, 1.0)
-exact = lax.Precision.HIGHEST
 
 parts = 6
 early = (2,)
@@ -123,10 +122,6 @@
     return right * scale
 
 
-def mul(a, b, contract):
-    return lax.dot_general(a, b, ((contract[0:1], contract[1:2]), ((), ())), precision=exact, preferred_element_type=jnp.float32)
-
-
 def dot16(a, b, contract):
     return lax.dot_general(a, b, ((contract[0:1], contract[1:2]), ((), ())), preferred_element_type=jnp.float32)
 
@@ -143,6 +138,13 @@
     rh, rm, rl = thirds(right)
     return dot16(
         jnp.concatenate([lh, lh, lm, lm, lh, ll], axis=0), jnp.concatenate([rh, rm, rh, rm, rl, rh], axis=0), (0, 0)
+    )
+
+
+def high_mul(left, right, contract):
+    (left_high, left_low), (right_high, right_low) = halves(left), halves(right)
+    return dot16(left_high, right_high, contract) + (
+        dot16(left_high, right_low, contract) + dot16(left_low, right_high, contract)
     )
 
 
@@ -501,9 +503,9 @@
         ],
         axis=0,
     )
-    middle = mul(upper, bar, (1, 1)) - mul(cross.T, inverse, (1, 1))
+    middle = high_mul(upper, bar, (1, 1)) - high_mul(cross.T, inverse, (1, 1))
     symmetric = jnp.where(row_ids >= col_ids, middle, middle.T)
-    mix = mul(inverse.T, mul(symmetric, inverse, (1, 0)), (1, 0))
+    mix = high_mul(inverse.T, high_mul(symmetric, inverse, (1, 0)), (1, 0))
     for begin, value in ((0, mix), (size, inverse)):
         lines = slice(begin, begin + size)
         high, rest = halves(value)
@@ -577,6 +579,40 @@
             sent(functools.partial(message, partial, False, 1, 1, piece))
 
 
+def place_kernel(z_ref, noise_ref, z_out, noise_out, held, load_sem, store_sem):
+    quads = z_ref.shape[0]
+    loads, stores = [], []
+    for index, (source, target) in enumerate(((z_ref, z_out), (noise_ref, noise_out))):
+        for quad in range(quads):
+            slot = index * quads + quad
+            loads.append(pltpu.make_async_copy(source.at[quad], held.at[slot], load_sem.at[slot]))
+            stores.append(pltpu.make_async_copy(held.at[slot], target.at[quad], store_sem.at[slot]))
+    for load in loads:
+        load.start()
+    for load, store in zip(loads, stores):
+        load.wait()
+        store.start()
+    for store in stores:
+        store.wait()
+
+
+def place(z_grad, noise_grad):
+    far = pl.BlockSpec(memory_space=pl.ANY)
+    count = 2 * z_grad.shape[0]
+    return pl.pallas_call(
+        place_kernel,
+        out_shape=tuple(jax.ShapeDtypeStruct(value.shape, value.dtype) for value in (z_grad, noise_grad)),
+        in_specs=[far, far],
+        out_specs=(far, far),
+        scratch_shapes=[
+            pltpu.VMEM((count,) + z_grad.shape[1:], jnp.float32),
+            pltpu.SemaphoreType.DMA((count,)),
+            pltpu.SemaphoreType.DMA((count,)),
+        ],
+        compiler_params=pltpu.CompilerParams(vmem_limit_bytes=62 * 2**20),
+    )(z_grad, noise_grad)
+
+
 def on_device(cell_coeffs, z_factor, noise_cols, q_bar, r_bar):
     count = lax.axis_size("row")
     quads, rows, cells, cols = z_factor.shape
@@ -594,7 +630,7 @@
     def shorts(*shape):
         return pltpu.VMEM(shape, jnp.bfloat16)
 
-    return pl.pallas_call(
+    z_grad, noise_grad = pl.pallas_call(
         functools.partial(whole_kernel, count),
         out_shape=(
             jax.ShapeDtypeStruct(z_factor.shape, jnp.float32),
@@ -636,6 +672,7 @@
             collective_id=0, has_side_effects=True, vmem_limit_bytes=62 * 2**20
         ),
     )(cell_coeffs, z_factor, noise_cols, q_bar, r_bar)
+    return place(z_grad, noise_grad)
 
 
 def solution(mesh):

time: 71.1 us -> 69.5 us (0.977)
  local copies, waits for them, and re-layouts: 3.93 us -> 0 us
  Pallas kernels: 66.4 us -> 68.6 us
    unnamed x4 -> x0, local copies, waits for them, and re-layouts: 3.93 us -> none
    pallas_call x0 -> x1, Pallas kernels: none -> 2.79 us  [place(): pl.pallas_call(place_kernel, out_shape=tuple((jax.ShapeDtypeStruct(value....]
where the time goes in v5:
time: 69.5 us; the launch traced here: 69.4 us
  Pallas kernels  68.6 us (99%)
  between operations  0.8 us (1%)
    pallas_call x1, Pallas kernels, on_device(): pl.pallas_call(functools.partial(whole_kernel, count), out_shape=(jax.Sha...  65.8 us
    pallas_call x1, Pallas kernels, place(): pl.pallas_call(place_kernel, out_shape=tuple((jax.ShapeDtypeStruct(value....  2.79 us

profile of v5, /device:TPU:9, one launch (start us, length us, event | category | flops | bytes accessed | tf_op | source)
XLA Modules:
  0.0 69.4 jit_solution(7609930242216418037)
XLA Ops:
  0.6 65.8 %shard_map.68 = (f32[4,2,384,128]{3,2,1,0:T(8,128)}, f32[4,2,384,128]{3,2,1,0:T(8,128)}) custom-call(f32[6,2,384]{2,1,0:T(2,128)} %coef_hbm.1, f32[4,2,384,128]{3,2,1,0:T(8,128)} %z_hbm.1, f32[4,2,384,128]{3,2,1,0:T(8,128)} %noise_hbm.1, f32[4,2,384,256]{3,2,1,0:T(8,128)} %bar_hbm.1, f32[256,256]{1,0:T(8,128)} %rbar_hbm.1), custom_call_target="tpu_custom_call" | custom-call | tf_op jit(solution)/shard_map/pallas_call | solution.py:633
  66.4 2.8 %shard_map.69 = (f32[4,2,384,128]{3,2,1,0:T(8,128)}, f32[4,2,384,128]{3,2,1,0:T(8,128)}) custom-call(f32[4,2,384,128]{3,2,1,0:T(8,128)} %get-tuple-element.4.z_ref, f32[4,2,384,128]{3,2,1,0:T(8,128)} %get-tuple-element.5.noise_ref), custom_call_target="tpu_custom_call" | custom-call | tf_op jit(solution)/shard_map/pallas_call | solution.py:602

commit v6 on v5

--- a/solution.py
+++ b/solution.py
@@ -11,7 +11,7 @@
 extra_scales = (1.0, 1.0, 2.0, 0.5, 0.5, 1.0)
 
 parts = 6
-early = (2,)
+early = (1,)
 margin = 8
 tile = 32
 
@@ -148,6 +148,14 @@
     )
 
 
+def packed_rows(left, right):
+    lh, lm, ll = thirds(left)
+    rh, rm, rl = thirds(right)
+    return dot16(
+        jnp.concatenate([lh, lh, lm, lm, lh, ll], axis=1), jnp.concatenate([rh, rm, rh, rm, rl, rh], axis=0), (1, 0)
+    )
+
+
 def halves(value):
     high = value.astype(jnp.bfloat16)
     return high, (value - high.astype(jnp.float32)).astype(jnp.bfloat16)
@@ -484,7 +492,7 @@
     for start in range(0, size, tile):
         stop = start + tile
         small = tile_inverse(work[start:stop, start:stop])
-        panel = packed(small.T, work[start:stop, :])
+        panel = packed_rows(small, work[start:stop, :])
         work[start:stop, :] = panel
         if stop < size:
             base, end = stop // 128 * 128, size + (stop + 127) // 128 * 128
@@ -510,7 +518,6 @@
         lines = slice(begin, begin + size)
         high, rest = halves(value)
         weight_z[lines, :cols], weight_z[lines, cols:] = high[:, :cols], rest[:, :cols]
-        weight_n[lines, :cols], weight_n[lines, cols:] = high[:, cols:], rest[:, cols:]
 
     def gradient(weight, piece):
         lines = slice(piece * block, (piece + 1) * block)
@@ -542,6 +549,9 @@
                 for plane in range(4):
                     halo[1, side, plane, at(piece)] = edge[plane * chunk : (plane + 1) * chunk]
 
+    for begin, value in ((0, mix), (size, inverse)):
+        lines = slice(begin, begin + size)
+        weight_n[lines, :cols], weight_n[lines, cols:] = halves(value[:, cols:])
     for piece in range(parts):
         grad = gradient(weight_n, piece)
         for quad in range(quads):

time: 69.5 us -> 69.4 us (level)
  no operation moved by 1% of the time
where the time goes in v6:
time: 69.4 us; the launch traced here: 69.3 us
  Pallas kernels  68.5 us (99%)
  between operations  0.8 us (1%)
    pallas_call x1, Pallas kernels, on_device(): pl.pallas_call(functools.partial(whole_kernel, count), out_shape=(jax.Sha...  65.7 us
    pallas_call x1, Pallas kernels, place(): pl.pallas_call(place_kernel, out_shape=tuple((jax.ShapeDtypeStruct(value....  2.79 us

profile of v6, /device:TPU:9, one launch (start us, length us, event | category | flops | bytes accessed | tf_op | source)
XLA Modules:
  0.0 69.3 jit_solution(16397850844057023183)
XLA Ops:
  0.6 65.7 %shard_map.68 = (f32[4,2,384,128]{3,2,1,0:T(8,128)}, f32[4,2,384,128]{3,2,1,0:T(8,128)}) custom-call(f32[6,2,384]{2,1,0:T(2,128)} %coef_hbm.1, f32[4,2,384,128]{3,2,1,0:T(8,128)} %z_hbm.1, f32[4,2,384,128]{3,2,1,0:T(8,128)} %noise_hbm.1, f32[4,2,384,256]{3,2,1,0:T(8,128)} %bar_hbm.1, f32[256,256]{1,0:T(8,128)} %rbar_hbm.1), custom_call_target="tpu_custom_call" | custom-call | tf_op jit(solution)/shard_map/pallas_call | solution.py:643
  66.3 2.8 %shard_map.69 = (f32[4,2,384,128]{3,2,1,0:T(8,128)}, f32[4,2,384,128]{3,2,1,0:T(8,128)}) custom-call(f32[4,2,384,128]{3,2,1,0:T(8,128)} %get-tuple-element.4.z_ref, f32[4,2,384,128]{3,2,1,0:T(8,128)} %get-tuple-element.5.noise_ref), custom_call_target="tpu_custom_call" | custom-call | tf_op jit(solution)/shard_map/pallas_call | solution.py:612
